TPU v7x, 32 devices: a whole 2x2x4 slice. The times are simulated.
32 devices in a mesh: facet: 4 (over y, core), sub: 8 (over z, x).
Axes of the slice: x: 2, y: 2, z: 4, core: 2. Of those that a mesh axis runs over, the one named last changes fastest.
Arguments:
- facet_data: bfloat16 [2, 16, 32768], P(None, None, ('facet', 'sub')), may hold values from -6 to 6
- subgrid_pos: int32 [32], P(('facet', 'sub')), may hold values from 0 to 32640, as said below
- vis_counts: int32 [32], P(('facet', 'sub')), may hold values from 128 to 512, as said below
- vis_u_fine: int32 [32, 512], P(('facet', 'sub')), may hold values from 0 to 8079
- vis_v_fine: int32 [32, 512], P(('facet', 'sub')), may hold values from 0 to 143
- vis_observed: float32 [2, 32, 512], P(None, ('facet', 'sub')), may hold values from -6 to 6
Outputs:
- vis_residual: float32 [2, 32, 512], P(None, ('facet', 'sub'))
- facet_residual: float32 [2, 16, 32768], P(None, None, ('facet', 'sub'))
Inputs may be any that keep to these rules, and one draw needn't show every extreme that they name: `subgrid_pos`: distinct multiples of 128; a subgrid's u cells o to o + 511 are taken modulo 32768. The first vis_counts[s] slots of subgrid s are live; some subgrid has all 512 slots live.
All inputs are finite; a program needn't handle non-finite values.
Results may differ from a plain program's by a relative error of at most 0.012.
Values may be sent and summed in bfloat16 or wider, within the bound.
A program may use at most 64 MiB of HBM per device.

v0:
```python
import math

import jax
import jax.numpy as jnp
from jax import lax
from jax.sharding import PartitionSpec as P

FW = 8192
SG = 512
KS = 8
OVER = 16


def phase_slot_index(left_side, right_side, image_width):
    right_high = right_side // 256
    right_low = right_side % 256
    return (
        left_side * right_low % image_width + left_side * right_high % image_width * 256
    ) % image_width


def phasor(phase_total_count, image_width):
    phase_angle = 2.0 * math.pi * (phase_total_count.astype(jnp.float32) / float(image_width))
    return (jnp.cos(phase_angle), jnp.sin(phase_angle))


def build_phase_tables(sub_width, image_width):
    table_range = jnp.arange(sub_width, dtype=jnp.int32)
    cosine, sine_part = phasor(
        phase_slot_index(table_range[:, None], table_range[None, :], image_width), image_width
    )
    norm_scale = 1.0 / math.sqrt(image_width)
    real_part = (cosine * norm_scale).astype(jnp.bfloat16)
    imag_part = (-sine_part * norm_scale).astype(jnp.bfloat16)
    forward_table = jnp.concatenate(
        [jnp.concatenate([real_part, imag_part], 1), jnp.concatenate([-imag_part, real_part], 1)], 0
    )
    backward_table = jnp.concatenate(
        [jnp.concatenate([real_part, -imag_part], 1), jnp.concatenate([imag_part, real_part], 1)], 0
    )
    return (forward_table, backward_table)


def forward_part(columns, positions, table, image_width):
    sub_width = table.shape[0] // 2
    rows_v = columns.shape[1]
    blocks = columns.shape[2] // sub_width
    inside = jnp.arange(sub_width, dtype=jnp.int32)
    mod_cos, mod_sin = phasor(
        phase_slot_index(inside[None, :], positions[:, None], image_width), image_width
    )
    mod_cos = mod_cos[:, None, None, :]
    mod_sin = mod_sin[:, None, None, :]
    image_band = columns.astype(jnp.float32).reshape(2, rows_v, blocks, sub_width)
    real_z = image_band[0][None] * mod_cos + image_band[1][None] * mod_sin
    imag_z = image_band[1][None] * mod_cos - image_band[0][None] * mod_sin
    stacked = jnp.concatenate([real_z, imag_z], -1).astype(jnp.bfloat16)
    partial_grid = jnp.dot(stacked, table, preferred_element_type=jnp.float32)
    anchors = jnp.arange(blocks, dtype=jnp.int32) * sub_width
    columns_u = (positions[:, None] + inside[None, :]) % image_width
    post_cos, post_sin = phasor(
        phase_slot_index(anchors[None, :, None], columns_u[:, None, :], image_width), image_width
    )
    post_cos = post_cos[:, None]
    post_sin = post_sin[:, None]
    real_p = partial_grid[..., :sub_width]
    imag_p = partial_grid[..., sub_width:]
    real_g = jnp.sum(real_p * post_cos + imag_p * post_sin, axis=2)
    imag_g = jnp.sum(imag_p * post_cos - real_p * post_sin, axis=2)
    return jnp.concatenate([real_g, imag_g], -1)


def kernel_weights(fine_index, cells):
    cell_index = fine_index // OVER
    frac_index = fine_index % OVER
    cell_range = jnp.arange(cells, dtype=jnp.int32)
    cell_offset = cell_range[None, None, :] - cell_index[..., None]
    distance = (
        cell_offset.astype(jnp.float32)
        - (KS - 1) / 2.0
        - frac_index.astype(jnp.float32)[..., None] / OVER
    )
    weight = jnp.exp(-0.5 * (distance / 0.6) ** 2)
    return jnp.where((cell_offset >= 0) & (cell_offset < KS), weight, jnp.float32(0.0))


def degrid_regrid(subgrid_data, u_fine, v_fine, counts, observed):
    sub_width = subgrid_data.shape[2] // 2
    weight_u = kernel_weights(u_fine, sub_width)
    kernel_weight_v = kernel_weights(v_fine, subgrid_data.shape[1])
    gridded_values = subgrid_data.astype(jnp.float32)
    along_v_axis = jnp.einsum(
        "jtz,jzh->jth", kernel_weight_v, gridded_values, precision=lax.Precision.HIGHEST
    )
    real_pred = jnp.sum(along_v_axis[..., :sub_width] * weight_u, -1)
    imag_pred = jnp.sum(along_v_axis[..., sub_width:] * weight_u, -1)
    slot_range = jnp.arange(u_fine.shape[1], dtype=jnp.int32)
    live_mask = slot_range[None, :] < counts[:, None]
    real_res = jnp.where(live_mask, observed[0] - real_pred, jnp.float32(0.0))
    imag_res = jnp.where(live_mask, observed[1] - imag_pred, jnp.float32(0.0))
    spread_onto_grid = jnp.concatenate(
        [real_res[..., None] * weight_u, imag_res[..., None] * weight_u], -1
    )
    regridded_values = jnp.einsum(
        "mlz,mlr->mzr", kernel_weight_v, spread_onto_grid, precision=lax.Precision.HIGHEST
    ).astype(jnp.bfloat16)
    return (jnp.stack([real_res, imag_res]), regridded_values)


def backward_part(grids, positions, x_start, span, table, image_width):
    sub_width = table.shape[0] // 2
    rows_v = grids.shape[1]
    blocks = span // sub_width
    inside = jnp.arange(sub_width, dtype=jnp.int32)
    anchors = x_start + jnp.arange(blocks, dtype=jnp.int32) * sub_width
    columns_u = (positions[:, None] + inside[None, :]) % image_width
    pre_cos, pre_sin = phasor(
        phase_slot_index(anchors[None, :, None], columns_u[:, None, :], image_width), image_width
    )
    pre_cos = pre_cos[:, None]
    pre_sin = pre_sin[:, None]
    real_h = grids[..., :sub_width].astype(jnp.float32)[:, :, None, :]
    imag_h = grids[..., sub_width:].astype(jnp.float32)[:, :, None, :]
    real_m = real_h * pre_cos - imag_h * pre_sin
    imag_m = real_h * pre_sin + imag_h * pre_cos
    stacked = jnp.concatenate([real_m, imag_m], -1).astype(jnp.bfloat16)
    product = jnp.dot(stacked, table, preferred_element_type=jnp.float32)
    mod_cos, mod_sin = phasor(
        phase_slot_index(inside[None, :], positions[:, None], image_width), image_width
    )
    mod_cos = mod_cos[:, None, None, :]
    mod_sin = mod_sin[:, None, None, :]
    real_q = product[..., :sub_width]
    imag_q = product[..., sub_width:]
    real_out = jnp.sum(real_q * mod_cos - imag_q * mod_sin, axis=0)
    imag_out = jnp.sum(real_q * mod_sin + imag_q * mod_cos, axis=0)
    return jnp.stack([real_out, imag_out]).reshape(2, rows_v, span)


def shards(facet_data, subgrid_pos, vis_counts, vis_u_fine, vis_v_fine, vis_observed):
    facets = lax.axis_size("facet")
    sub_count = lax.axis_size("sub")
    image_width = FW * facets
    columns = facet_data.shape[2]
    device_place = lax.axis_index("facet") * sub_count + lax.axis_index("sub")
    x_begin = device_place * columns
    forward_table, backward_table = build_phase_tables(SG, image_width)
    summed = forward_part(
        lax.all_gather(facet_data, ("facet", "sub"), axis=2, tiled=True),
        subgrid_pos,
        forward_table,
        image_width,
    )
    subgrid_data = summed.astype(jnp.bfloat16)
    residual, regridded_values = degrid_regrid(
        subgrid_data, vis_u_fine, vis_v_fine, vis_counts, vis_observed
    )
    residual_image = backward_part(
        lax.all_gather(regridded_values, ("facet", "sub"), axis=0, tiled=True),
        lax.all_gather(subgrid_pos, ("facet", "sub"), axis=0, tiled=True),
        x_begin,
        columns,
        backward_table,
        image_width,
    )
    return (residual, residual_image)


def solution(mesh):
    return jax.shard_map(
        shards,
        mesh=mesh,
        in_specs=(
            P(None, None, ("facet", "sub")),
            P(("facet", "sub")),
            P(("facet", "sub")),
            P(("facet", "sub"), None),
            P(("facet", "sub"), None),
            P(None, ("facet", "sub"), None),
        ),
        out_specs=(P(None, ("facet", "sub"), None), P(None, None, ("facet", "sub"))),
        check_vma=False,
    )
```

profile of v0, /device:TPU:0, one launch (start us, length us, event | category | flops | bytes accessed | tf_op | source)
XLA Modules:
  0.0 148.4 jit_solution(17813533866015794701)
XLA Ops:
  7.2 0.7 all-gather.4.cloned.1.call-update
  9.4 0.7 and_select_fusion.6
  10.1 0.7 and_select_fusion.4
  10.8 0.7 fusion.69
  11.5 4.9 %fusion.53 = bf16[512,512]{1,0:T(8,128)(2,1)S(1)} fusion(s32[512]{0:T(512)S(1)} %get-tuple-element.38, s32[512]{0:T(512)S(1)} %get-tuple-element.39), kind=kLoop, calls=%fused_computation.131 | loop fusion | flops 11796480 | bytes 528384 | tf_op jit(solution)/shard_map/neg | solution.py:36
  16.4 5.2 %multiply_convert_fusion = (bf16[512,512]{1,0:T(8,128)(2,1)S(1)}, bf16[512,512]{1,0:T(8,128)(2,1)S(1)}) fusion(s32[512]{0:T(512)S(1)} %get-tuple-element.38, s32[512]{0:T(512)S(1)} %get-tuple-element.39), kind=kLoop, calls=%fused_computation.68 | loop fusion | flops 11534336 | bytes 1052672 | tf_op jit(solution)/shard_map/convert_element_type | solution.py:34
  21.6 48.4 %all-gather.4.cloned.1.call-done = bf16[2,16,32768]{2,1,0:T(8,128)(2,1)} async-done(((bf16[2,16,1024]{2,1,0:T(8,128)(2,1)}), bf16[2,16,32768]{2,1,0:T(8,128)(2,1)}) %all-gather.4.cloned.1.call-update) | async-done | bytes 2097168 | tf_op jit(solution)/shard_map/all_gather | solution.py:149
  70.0 1.8 %fusion.137 = (f32[1,16,32768]{2,1,0:T(8,128)S(1)}, f32[1,16,32768]{2,1,0:T(8,128)S(1)}) fusion(bf16[2,16,32768]{2,1,0:T(8,128)(2,1)} %all-gather.4.cloned.1.call-done), kind=kLoop, calls=%fused_computation.265 | loop fusion | bytes 8388608 | tf_op jit(solution)/shard_map/slice | solution.py:55
  71.8 1.2 copy.14
  73.1 1.2 copy.13
  74.3 0.7 fusion.8
  75.0 2.3 %convolution_bitcast_fusion = f32[1,16,64,1024]{3,2,1,0:T(8,128)S(1)} fusion(bf16[512,512]{1,0:T(8,128)(2,1)S(1)} %get-tuple-element.31, bf16[16,64,512]{2,1,0:T(8,128)(2,1)S(1)} %get-tuple-element.13, bf16[16,64,512]{2,1,0:T(8,128)(2,1)S(1)} %get-tuple-element.12, bf16[512,512]{1,0:T(8,128)(2,1)S(1)} %fusion.53, bf16[512,512]{1,0:T(8,128)(2,1)S(1)} %get-tuple-element.30), kind=kOutput, calls=%fused_computation.4 | convolution fusion | flops 2160066560 | bytes 7864320 | tf_op jit(solution)/shard_map/dot_general | solution.py:58
  77.3 0.7 add_reduce_fusion.1
  78.0 1.0 convolution_bitcast_fusion.1
  79.1 0.8 fusion.35
  80.6 1.8 %fusion.26 = bf16[16,1024]{1,0:T(8,128)(2,1)} fusion(f32[1,512,512]{2,1,0:T(8,128)S(1)} %get-tuple-element.25, f32[1,512,512]{2,1,0:T(8,128)S(1)} %get-tuple-element.24, f32[512]{0:T(512)S(1)} %bitcast.71, s32[512]{0:T(512)S(1)} %bitcast.67), kind=kOutput, calls=%fused_computation.52 | convolution fusion | flops 101294080 | bytes 2134016 | tf_op jit(solution)/shard_map/mlz,mlr->mzr/dot_general | solution.py:104
  82.5 39.1 %all-reduce = s32[32]{0:T(128)S(1)} all-reduce(s32[32]{0:T(128)S(1)} %dynamic-update-slice), channel_id=1, replica_groups=mesh['facet'=4,'sub'=8] {'facet','sub'}, use_global_device_ids=true, to_apply=%add | all-reduce | flops 32 | bytes 256
  122.2 2.8 %fusion.100 = (f32[32,2,512]{2,1,0:T(2,128)S(1)}, f32[32,2,512]{2,1,0:T(2,128)S(1)}) fusion(s32[32,512]{1,0:T(8,128)S(1)} %get-tuple-element.37, s32[32,512]{1,0:T(8,128)S(1)} %get-tuple-element.36, s32[2]{0:T(128)S(1)} %multiply_add_fusion), kind=kLoop, calls=%fused_computation.185 | loop fusion | flops 1277952 | bytes 393224 | tf_op jit(solution)/shard_map/cos | solution.py:24
  125.6 9.7 %all-gather.6.cloned.1.call-done = bf16[512,1024]{1,0:T(8,128)(2,1)} async-done(((bf16[16,1024]{1,0:T(8,128)(2,1)}), bf16[512,1024]{1,0:T(8,128)(2,1)}) %all-gather.6.cloned.1.call-update) | async-done | bytes 1048592 | tf_op jit(solution)/shard_map/all_gather | solution.py:159
  135.4 1.5 slice_convert_fusion.1
  136.9 0.8 subtract_convert_fusion
  137.7 2.3 %fusion.5 = f32[32,16,2,1024]{3,1,2,0:T(8,128)S(1)} fusion(bf16[512,512]{1,0:T(8,128)(2,1)S(1)} %get-tuple-element.31, bf16[32,16,2,512]{3,1,2,0:T(8,128)(2,1)S(1)} %get-tuple-element.15, bf16[32,16,2,512]{3,1,2,0:T(8,128)(2,1)S(1)} %get-tuple-element.14, bf16[512,512]{1,0:T(8,128)(2,1)S(1)} %get-tuple-element.30, bf16[512,512]{1,0:T(8,128)(2,1)S(1)} %fusion.53), kind=kOutput, calls=%fused_computation.9 | convolution fusion | flops 2160066560 | bytes 7864320 | tf_op jit(solution)/shard_map/dot_general | solution.py:127
  140.0 0.7 subtract_reduce_fusion
  140.9 0.7 pad_maximum_fusion.6
  (26 shorter events, 2.4 us)
Async XLA Ops:
  7.2 62.9 %all-gather.4.cloned.1.call-start = ((), (), s32[]{:S(2)}) async-start(), calls=%async_computation | async-start | bytes 2162688 | tf_op jit(solution)/shard_map/all_gather | solution.py:149
  7.9 127.5 %all-gather.6.cloned.1.call-start = ((), (), s32[]{:S(2)}) async-start(), calls=%async_computation.1 | async-start | bytes 1081344 | tf_op jit(solution)/shard_map/all_gather | solution.py:159
  78.0 1.9 %copy-start = (f32[2,1,512]{2,1,0:T(1,128)S(1)}, f32[2,1,512]{2,1,0:T(1,128)}, u32[]{:S(2)}) copy-start(f32[2,1,512]{2,1,0:T(1,128)} %param.11) | copy-start | bytes 12292
Sparse Core Ops, SparseCore 0:
  11.1 58.9 all-gather.3
  82.5 52.8 all-gather.5
where the time goes:
time: 149 us; the launch traced here: 148 us
  waiting for transfers between devices  58.9 us (40%)
  blocking collectives  39.1 us (26%)
  other arithmetic  22.7 us (15%)
  between operations  15.6 us (10%)
  matrix products  7.46 us (5%)
  local copies, waits for them, and re-layouts  4.6 us (3%)
    all_gather x1, waiting for transfers between devices, shards(): lax.all_gather(facet_data, ('facet', 'sub'), axis=2, tiled=True)  48.4 us
    unnamed x1, blocking collectives  39.1 us
    all_gather x1, waiting for transfers between devices, shards(): lax.all_gather(regridded_values, ('facet', 'sub'), axis=0, tiled=True)  9.74 us
    convert_element_type x1, other arithmetic, build_phase_tables(): imag_part = (-sine_part * norm_scale).astype(jnp.bfloat16)  5.21 us
    neg x1, other arithmetic, build_phase_tables(): -imag_part  4.87 us
    cos x3, other arithmetic, phasor(): return (jnp.cos(phase_angle), jnp.sin(phase_angle))  3.93 us
  transfers between devices with their start and end apart: 2, of which 2 were waited for; matrix products, arithmetic and copies ran while one was open for 11% of the time, Pallas kernels for 0%

commit v1 on v0

v1 whole, which is shorter than its diff:
```python
import functools
import math

import jax
import jax.numpy as jnp
import numpy as np
from jax import lax
from jax.experimental import pallas as pl
from jax.experimental.pallas import tpu as pltpu
from jax.sharding import PartitionSpec as P

SG = 512
KS = 8
OVER = 16
MESH = pl.DeviceIdType.MESH
F32 = jnp.float32
BF16 = jnp.bfloat16


class Plan:
    def __init__(self, devices, nsub, rows_v, columns):
        self.devices = devices
        self.nsub = nsub
        self.rows_v = rows_v
        self.width = columns * devices
        self.nb = self.width // SG
        self.rl = self.nb // devices
        self.times = SG // self.nb
        self.vg = min(rows_v, devices // 4)
        self.xg = devices // self.vg
        self.v2 = rows_v // self.vg
        self.xl = SG // self.xg
        self.used = self.rl * self.v2
        self.q = self.vg * 8
        self.x = self.xg * 128
        self.extra = 2 * self.xg


def block_transform(plan):
    ids = np.arange(plan.nb)
    angle = 2.0 * np.pi * ((ids[:, None] * ids[None, :]) % plan.nb) / plan.nb
    cosine = np.cos(angle).reshape(plan.devices, plan.rl, plan.devices, plan.rl)
    sine = np.sin(angle).reshape(plan.devices, plan.rl, plan.devices, plan.rl)
    table = np.zeros((plan.devices, 2, 4, plan.devices, 2, 4), np.float32)
    for i in range(plan.rl):
        for k in range(plan.rl):
            for v in range(plan.v2):
                out, into = i * plan.v2 + v, k * plan.v2 + v
                table[:, 0, out, :, 0, into] = cosine[:, i, :, k]
                table[:, 0, out, :, 1, into] = sine[:, i, :, k]
                table[:, 1, out, :, 0, into] = -sine[:, i, :, k]
                table[:, 1, out, :, 1, into] = cosine[:, i, :, k]
    return table.reshape(plan.devices * 8, plan.devices * 8)


def turn_table(plan):
    lane = np.arange(plan.x)
    x = (lane // 128) * plan.xl + lane % 128
    angle = 2.0 * np.pi * ((np.arange(8)[:, None] * x[None, :]) % SG) / SG
    return np.cos(angle).astype(np.float32), np.sin(angle).astype(np.float32)


def nt(a, b):
    return lax.dot_general(a, b, (((1,), (1,)), ((), ())), preferred_element_type=F32)


def tn(a, b):
    return lax.dot_general(a, b, (((0,), (0,)), ((), ())), preferred_element_type=F32)


def split(a):
    high = a.astype(BF16)
    return high, (a - high.astype(F32)).astype(BF16)


def swapped(a):
    row = lax.broadcasted_iota(jnp.int32, a.shape, 1)
    turned = pltpu.roll(a, 4, 1)
    return jnp.where(row < 4, turned, -turned)


def kernel(
    plan, prep, u_fine, v_fine, observed, count, high, low, back, turn_c, turn_s,
    res_out, image_out,
    r_a, s_b, r_b, s_c, r_c, s_d, r_d, s_e, r_e, s_f, r_f,
    wu, tch, tcl, tsh, tsl, send_sem, recv_sem,
):
    devices, nsub = plan.devices, plan.nsub
    me = lax.axis_index("facet") * nsub + lax.axis_index("sub")

    def place(i):
        target = lax.rem(me + i, devices)
        return target, (target // nsub, lax.rem(target, nsub))

    barrier = pltpu.get_barrier_semaphore()

    def greet(i, carry):
        pl.semaphore_signal(barrier, inc=1, device_id=place(i)[1], device_id_type=MESH)
        return carry

    lax.fori_loop(1, devices, greet, 0)
    pl.semaphore_wait(barrier, devices - 1)

    def send(phase, source, target):
        def one(i, carry):
            to, device = place(i)
            pltpu.make_async_remote_copy(
                src_ref=source.at[to],
                dst_ref=target.at[me],
                send_sem=send_sem.at[phase],
                recv_sem=recv_sem.at[phase],
                device_id=device,
                device_id_type=MESH,
            ).start()
            return carry

        lax.fori_loop(1, devices, one, 0)
        target[me] = source[me]

    def wait(sem, phase, target):
        others = target.at[pl.ds(0, devices - 1)]
        pltpu.make_async_copy(others, others, sem.at[phase]).wait()

    send(0, prep, r_a)

    cu = u_fine[...] // OVER
    shift = (KS - 1) / 2.0 + (u_fine[...] % OVER).astype(F32) / OVER
    half = devices * 8
    for i in range(plan.rl):
        row = lax.broadcasted_iota(jnp.int32, (half, u_fine.shape[1]), 0)
        cell = plan.nb * (row % 8) + (row // 8) * plan.rl + i
        offset = cell - cu
        distance = (offset.astype(F32) - shift) / 0.6
        weight = jnp.exp(-0.5 * distance * distance)
        weight = jnp.where((offset >= 0) & (offset < KS), weight, 0.0)
        wu[pl.ds(i * half, half), :] = weight.astype(BF16)

    shape = (plan.q, v_fine.shape[1])
    row = lax.broadcasted_iota(jnp.int32, shape, 0)
    offset = (row // 8) * plan.v2 + (row % 4) % plan.v2 - v_fine[...] // OVER
    shift = (KS - 1) / 2.0 + (v_fine[...] % OVER).astype(F32) / OVER
    distance = (offset.astype(F32) - shift) / 0.6
    wv = jnp.exp(-0.5 * distance * distance)
    wv = jnp.where((offset >= 0) & (offset < KS), wv, 0.0)

    row = lax.broadcasted_iota(jnp.int32, (8, plan.x), 0)
    lane = lax.broadcasted_iota(jnp.int32, (8, plan.x), 1)
    x = (lane // 128) * plan.xl + lane % 128
    r = me * plan.rl + (row % 4) // plan.v2
    angle = (2.0 * math.pi / plan.width) * ((x * r) % plan.width).astype(F32)
    scale = 1.0 / math.sqrt(plan.width)
    tw_c = (jnp.cos(angle) * scale)[None]
    tw_s = (jnp.sin(angle) * scale)[None]

    wait(recv_sem, 0, r_a)

    data = r_a[:, 0:8, :].reshape(half, 128).astype(BF16)
    total = jnp.dot(high[...], data, preferred_element_type=F32)
    total += jnp.dot(low[...], data, preferred_element_type=F32)
    s_b[...] = total.reshape(devices, 8, 128)
    send(1, s_b, r_b)

    for g in range(plan.xg):
        lanes = pl.ds(g * 128, 128)
        base_c = r_a[:, 8 + g : 9 + g, :]
        base_s = r_a[:, 8 + plan.xg + g : 9 + plan.xg + g, :]
        tc = base_c * turn_c[:, lanes][None] - base_s * turn_s[:, lanes][None]
        ts = base_s * turn_c[:, lanes][None] + base_c * turn_s[:, lanes][None]
        tch[:, lanes], tcl[:, lanes] = split(tc.reshape(half, 128))
        tsh[:, lanes], tsl[:, lanes] = split(ts.reshape(half, 128))

    wait(recv_sem, 1, r_b)

    got = r_b[...].reshape(plan.vg, plan.xg, 8, 128)
    a = jnp.concatenate([got[:, g] for g in range(plan.xg)], axis=2)
    a = a * tw_c + swapped(a) * tw_s
    a_h, a_l = split(a.reshape(plan.q, plan.x))
    w_h, w_l = split(swapped(a).reshape(plan.q, plan.x))
    grid = nt(tch[...], a_h) + nt(tsh[...], w_h)
    grid += nt(tch[...], a_l) + nt(tsh[...], w_l)
    grid += nt(tcl[...], a_h) + nt(tsl[...], w_h)
    s_c[...] = grid.reshape(devices, 8, plan.q)
    send(2, s_c, r_c)
    wait(recv_sem, 2, r_c)

    cells = r_c[...].reshape(half, plan.q)
    column = lax.broadcasted_iota(jnp.int32, (half, plan.q), 1)
    residue = (column % 4) // plan.v2
    parts = [jnp.where(residue == i, cells, 0.0) for i in range(plan.rl)]
    cells = jnp.concatenate(parts, axis=0).astype(BF16)
    along = tn(cells, wu[...]) * wv
    along = jnp.sum(along.reshape(plan.vg, 8, -1), axis=0)
    live = lax.broadcasted_iota(jnp.int32, (1, shape[1]), 1) < count[...]
    real = jnp.where(live, observed[0:1, :] - jnp.sum(along[0:4], axis=0, keepdims=True), 0.0)
    imag = jnp.where(live, observed[1:2, :] - jnp.sum(along[4:8], axis=0, keepdims=True), 0.0)
    res_out[0:1, :] = real
    res_out[1:2, :] = imag
    row = lax.broadcasted_iota(jnp.int32, shape, 0)
    spread = (wv * jnp.where(row % 8 < 4, real, imag)).astype(BF16)
    both = nt(wu[...], spread)
    regrid = both[0:half]
    for i in range(1, plan.rl):
        regrid = jnp.where(residue == i, both[i * half : (i + 1) * half], regrid)
    s_d[...] = regrid.astype(BF16).astype(F32).reshape(devices, 8, plan.q)
    send(3, s_d, r_d)
    wait(recv_sem, 3, r_d)

    cells = r_d[...].reshape(half, plan.q).astype(BF16)
    first = tn(cells, tch[...]).reshape(plan.vg, 8, plan.x)
    second = tn(cells, tsh[...]).reshape(plan.vg, 8, plan.x)
    a = first - swapped(second)
    a = a * tw_c - swapped(a) * tw_s
    parts = [a[:, None, :, g * 128 : (g + 1) * 128] for g in range(plan.xg)]
    s_e[...] = jnp.concatenate(parts, axis=1).reshape(devices, 8, 128)
    send(4, s_e, r_e)
    wait(recv_sem, 4, r_e)

    data = r_e[...].reshape(half, 128).astype(BF16)
    total = jnp.dot(back[...], data, preferred_element_type=F32)
    s_f[...] = total.reshape(devices, 8, 128)
    send(5, s_f, r_f)
    wait(recv_sem, 5, r_f)
    image_out[...] = r_f[...]

    for phase, sent in enumerate((r_a, r_b, r_c, r_d, r_e, r_f)):
        wait(send_sem, phase, sent)


def shards(facet_data, subgrid_pos, vis_counts, vis_u_fine, vis_v_fine, vis_observed):
    nsub = lax.axis_size("sub")
    devices = lax.axis_size("facet") * nsub
    plan = Plan(devices, nsub, facet_data.shape[1], facet_data.shape[2])
    slots = vis_u_fine.shape[1]

    image = facet_data.astype(F32).reshape(2, plan.vg, plan.v2, plan.rl, plan.xg, plan.xl)
    image = image.transpose(1, 4, 0, 3, 2, 5).reshape(devices, 2, plan.used, plan.xl)
    image = jnp.pad(image, ((0, 0), (0, 0), (0, 4 - plan.used), (0, 128 - plan.xl)))
    x = jnp.arange(SG, dtype=jnp.int32)
    angle = (2.0 * math.pi / SG) * ((x * (subgrid_pos[0] // plan.nb)) % SG).astype(F32)
    base = jnp.stack([jnp.cos(angle), jnp.sin(angle)]).reshape(plan.extra, plan.xl)
    base = jnp.pad(base, ((0, 0), (0, 128 - plan.xl)))
    base = jnp.broadcast_to(base[None], (devices, plan.extra, 128))
    prep = jnp.concatenate([image.reshape(devices, 8, 128), base], axis=1)

    table = block_transform(plan)
    high = table.astype(BF16)
    low = (table - high.astype(np.float32)).astype(BF16)
    turn_c, turn_s = turn_table(plan)

    first = pltpu.VMEM((devices, 8 + plan.extra, 128), F32)
    tile = pltpu.VMEM((devices, 8, 128), F32)
    cell = pltpu.VMEM((devices, 8, plan.q), F32)
    turn = pltpu.VMEM((devices * 8, plan.x), BF16)
    residual, out = pl.pallas_call(
        functools.partial(kernel, plan),
        out_shape=(
            jax.ShapeDtypeStruct((2, slots), F32),
            jax.ShapeDtypeStruct((devices, 8, 128), F32),
        ),
        in_specs=[pl.BlockSpec(memory_space=pltpu.VMEM)] * 10,
        out_specs=(pl.BlockSpec(memory_space=pltpu.VMEM),) * 2,
        scratch_shapes=[
            first, tile, tile, cell, cell, cell, cell, tile, tile, tile, tile,
            pltpu.VMEM((plan.rl * devices * 8, slots), BF16),
            turn, turn, turn, turn,
            pltpu.SemaphoreType.DMA((6,)),
            pltpu.SemaphoreType.DMA((6,)),
        ],
        compiler_params=pltpu.CompilerParams(
            collective_id=0, has_side_effects=True, vmem_limit_bytes=48 * 1024 * 1024
        ),
    )(
        prep, vis_u_fine, vis_v_fine, vis_observed[:, 0], vis_counts.reshape(1, 1),
        jnp.asarray(high), jnp.asarray(low), jnp.asarray(high.T), turn_c, turn_s,
    )
    out = out.reshape(plan.vg, plan.xg, 2, 4, 128)[:, :, :, : plan.used, : plan.xl]
    out = out.reshape(plan.vg, plan.xg, 2, plan.rl, plan.v2, plan.xl)
    out = out.transpose(2, 0, 4, 3, 1, 5).reshape(facet_data.shape)
    return residual[:, None, :], out


def solution(mesh):
    return jax.shard_map(
        shards,
        mesh=mesh,
        in_specs=(
            P(None, None, ("facet", "sub")),
            P(("facet", "sub")),
            P(("facet", "sub")),
            P(("facet", "sub"), None),
            P(("facet", "sub"), None),
            P(None, ("facet", "sub"), None),
        ),
        out_specs=(P(None, ("facet", "sub"), None), P(None, None, ("facet", "sub"))),
        check_vma=False,
    )
```

time: 149 us -> 49.9 us (0.33)
  waiting for transfers between devices: 58.9 us -> 0 us
  Pallas kernels: 0 us -> 44.5 us
  blocking collectives: 39.1 us -> 0 us
  other arithmetic: 22.7 us -> 0.13 us
  between operations: 15.6 us -> 2.14 us
  matrix products: 7.46 us -> 0 us
  local copies, waits for them, and re-layouts: 4.6 us -> 2.93 us
    all_gather x2 -> x0, waiting for transfers between devices: 58.2 us -> none  [the longest x1 48.4 us: shards(): lax.all_gather(facet_data, ('facet', 'sub'), axis=2, tiled=True)]
    pallas_call x0 -> x1, Pallas kernels: none -> 44.5 us  [shards(): pl.pallas_call(functools.partial(kernel, plan), out_shape=(jax.ShapeDtype...]
    unnamed x1 -> x0, blocking collectives: 39.1 us -> none
    dot_general x4 -> x0, matrix products: 7.46 us -> none  [the longest x1 2.33 us: backward_part(): product = jnp.dot(stacked, table, preferred_element_type=jnp.float32)]
    convert_element_type x2 -> x0, other arithmetic: 6.68 us -> none  [the longest x1 5.21 us: build_phase_tables(): imag_part = (-sine_part * norm_scale).astype(jnp.bfloat16)]
    neg x1 -> x0, other arithmetic: 4.87 us -> none  [build_phase_tables(): -imag_part]
    cos x3 -> x0, other arithmetic: 3.93 us -> none  [phasor(): return (jnp.cos(phase_angle), jnp.sin(phase_angle))]
    another operation x4 -> x1, other arithmetic: 2.8 us -> 0.01 us  [shards(): jnp.stack([jnp.cos(angle), jnp.sin(angle)]).reshape(plan.extra, plan.xl)]
  transfers between devices with their start and end apart: 2 -> 0, of which waited for: 2 -> 0; matrix products, arithmetic and copies ran while one was open for 11% -> 0% of each run, Pallas kernels for 0% -> 0%
where the time goes in v1:
time: 49.9 us; the launch traced here: 49.7 us
  Pallas kernels  44.5 us (89%)
  local copies, waits for them, and re-layouts  2.93 us (6%)
  between operations  2.14 us (4%)
    pallas_call x1, Pallas kernels, shards(): pl.pallas_call(functools.partial(kernel, plan), out_shape=(jax.ShapeDtype...  44.5 us
    unnamed x20, local copies, waits for them, and re-layouts  2.04 us

profile of v1, /device:TPU:0, one launch (start us, length us, event | category | flops | bytes accessed | tf_op | source)
XLA Modules:
  0.0 49.7 jit_solution(4987393444552106281)
XLA Ops:
  1.3 0.1 fusion.3
  1.4 0.0 copy-start.7
  1.4 0.8 %copy-done.7 = bf16[2,16,1024]{2,1,0:T(8,128)(2,1)S(1)} copy-done((bf16[2,16,1024]{2,1,0:T(8,128)(2,1)S(1)}, bf16[2,16,1024]{2,1,0:T(8,128)(2,1)}, u32[]{:S(2)}) %copy-start.7) | copy-done | bytes 65560
  2.3 0.1 reshape.87
  2.3 0.1 copy.13
  2.4 0.0 copy-start.8
  2.4 0.0 copy-start
  2.4 0.0 copy-start.1
  2.4 0.0 copy-start.2
  2.4 0.0 copy-start.3
  2.5 0.0 copy-start.4
  2.5 0.6 %copy-done.8 = f32[2,1,512]{2,1,0:T(1,128)S(1)} copy-done((f32[2,1,512]{2,1,0:T(1,128)S(1)}, f32[2,1,512]{2,1,0:T(1,128)}, u32[]{:S(2)}) %copy-start.8) | copy-done | bytes 4120
  3.1 0.0 copy-start.6
  3.1 0.0 copy-start.5
  3.8 0.0 copy-done
  3.8 0.0 copy-done.1
  3.8 0.0 copy-done.2
  3.8 0.0 copy-done.3
  3.8 0.0 copy-done.4
  3.8 0.0 copy-done.6
  3.8 0.0 copy-done.5
  3.8 44.5 %shard_map.122 = (f32[2,512]{1,0:T(2,128)S(1)}, f32[32,8,128]{2,1,0:T(8,128)S(1)}) custom-call(f32[32,16,128]{2,1,0:T(8,128)S(1)} %pad_maximum_fusion.prep, s32[1,512]{1,0:T(1,128)S(1)} %copy-done.5, s32[1,512]{1,0:T(1,128)S(1)} %copy-done.6, f32[2,512]{1,0:T(2,128)S(1)} %bitcast.18, s32[1,1]{1,0:T(1,128)} %bitcast.16.count, bf16[256,256]{1,0:T(8,128)(2,1)S(1)} %copy-done, ...), custom_call_target="tpu_custom_call" | custom-call | tf_op jit(solution)/shard_map/pallas_call | solution.py:254
  48.4 0.7 %reshape.82 = f32[2,16,1024]{2,1,0:T(8,128)} reshape(f32[2,8,2,2,4,128]{5,4,3,2,1,0:T(4,128)S(1)} %copy.14) | data formatting | bytes 262144 | tf_op jit(solution)/shard_map/reshape | solution.py:278
  49.1 0.6 %copy.15 = f32[2,1,512]{2,1,0:T(1,128)} copy(f32[2,1,512]{2,0,1:T(2,128)S(1)} %bitcast.19) | data formatting | bytes 8192
  (6 shorter events, 0.1 us)
Async XLA Ops:
  1.4 0.8 %copy-start.7 = (bf16[2,16,1024]{2,1,0:T(8,128)(2,1)S(1)}, bf16[2,16,1024]{2,1,0:T(8,128)(2,1)}, u32[]{:S(2)}) copy-start(bf16[2,16,1024]{2,1,0:T(8,128)(2,1)} %param.11) | copy-start | bytes 196612
  2.4 0.7 %copy-start.8 = (f32[2,1,512]{2,1,0:T(1,128)S(1)}, f32[2,1,512]{2,1,0:T(1,128)}, u32[]{:S(2)}) copy-start(f32[2,1,512]{2,1,0:T(1,128)} %param.16) | copy-start | bytes 12292
  2.4 1.4 %copy-start = (bf16[256,256]{1,0:T(8,128)(2,1)S(1)}, bf16[256,256]{1,0:T(8,128)(2,1)}, u32[]{:S(2)}) copy-start(bf16[256,256]{1,0:T(8,128)(2,1)} %constant.43.clone.high) | copy-start | bytes 393220
  2.4 1.4 %copy-start.1 = (bf16[256,256]{1,0:T(8,128)(2,1)S(1)}, bf16[256,256]{1,0:T(8,128)(2,1)}, u32[]{:S(2)}) copy-start(bf16[256,256]{1,0:T(8,128)(2,1)} %constant.44.clone.low) | copy-start | bytes 393220
  2.4 1.4 %copy-start.2 = (bf16[256,256]{1,0:T(8,128)(2,1)S(1)}, bf16[256,256]{1,0:T(8,128)(2,1)}, u32[]{:S(2)}) copy-start(bf16[256,256]{1,0:T(8,128)(2,1)} %constant.45.clone.back) | copy-start | bytes 393220
  2.4 1.4 %copy-start.3 = (f32[8,512]{1,0:T(8,128)S(1)}, f32[8,512]{1,0:T(8,128)}, u32[]{:S(2)}) copy-start(f32[8,512]{1,0:T(8,128)} %constant.46.clone.turn_c) | copy-start | bytes 49156
  2.5 1.4 %copy-start.4 = (f32[8,512]{1,0:T(8,128)S(1)}, f32[8,512]{1,0:T(8,128)}, u32[]{:S(2)}) copy-start(f32[8,512]{1,0:T(8,128)} %constant.47.clone.turn_s) | copy-start | bytes 49156
  3.1 0.7 %copy-start.6 = (s32[1,512]{1,0:T(1,128)S(1)}, s32[1,512]{1,0:T(1,128)}, u32[]{:S(2)}) copy-start(s32[1,512]{1,0:T(1,128)} %v_fine.1) | copy-start | bytes 6148
  3.1 0.7 %copy-start.5 = (s32[1,512]{1,0:T(1,128)S(1)}, s32[1,512]{1,0:T(1,128)}, u32[]{:S(2)}) copy-start(s32[1,512]{1,0:T(1,128)} %u_fine.1) | copy-start | bytes 6148

commit v2 on v1

v2 whole, which is shorter than its diff:
```python
import functools
import math

import jax
import jax.numpy as jnp
import numpy as np
from jax import lax
from jax.experimental import pallas as pl
from jax.experimental.pallas import tpu as pltpu
from jax.sharding import PartitionSpec as P

SG = 512
KS = 8
OVER = 16
MESH = pl.DeviceIdType.MESH
F32 = jnp.float32
BF16 = jnp.bfloat16
COSINE = [(-1) ** k / math.factorial(2 * k) for k in range(9)]
SINE = [(-1) ** k / math.factorial(2 * k + 1) for k in range(8)]


class Plan:
    def __init__(self, devices, nsub, rows_v, columns):
        self.devices = devices
        self.nsub = nsub
        self.rows_v = rows_v
        self.width = columns * devices
        self.nb = self.width // SG
        self.rl = self.nb // devices
        self.times = SG // self.nb
        self.vg = min(rows_v, devices // 4)
        self.xg = devices // self.vg
        self.v2 = rows_v // self.vg
        self.xl = SG // self.xg
        self.used = self.rl * self.v2
        self.q = self.vg * 8
        self.x = self.xg * 128


def block_transform(plan):
    ids = np.arange(plan.nb)
    angle = 2.0 * np.pi * ((ids[:, None] * ids[None, :]) % plan.nb) / plan.nb
    cosine = np.cos(angle).reshape(plan.devices, plan.rl, plan.devices, plan.rl)
    sine = np.sin(angle).reshape(plan.devices, plan.rl, plan.devices, plan.rl)
    table = np.zeros((plan.devices, 2, 4, plan.devices, 2, 4), np.float32)
    for i in range(plan.rl):
        for k in range(plan.rl):
            for v in range(plan.v2):
                out, into = i * plan.v2 + v, k * plan.v2 + v
                table[:, 0, out, :, 0, into] = cosine[:, i, :, k]
                table[:, 0, out, :, 1, into] = sine[:, i, :, k]
                table[:, 1, out, :, 0, into] = -sine[:, i, :, k]
                table[:, 1, out, :, 1, into] = cosine[:, i, :, k]
    return table.reshape(plan.devices * 8, plan.devices * 8)


def nt(a, b):
    return lax.dot_general(a, b, (((1,), (1,)), ((), ())), preferred_element_type=F32)


def tn(a, b):
    return lax.dot_general(a, b, (((0,), (0,)), ((), ())), preferred_element_type=F32)


def split(a):
    high = a.astype(BF16)
    return high, (a - high.astype(F32)).astype(BF16)


def swapped(a):
    row = lax.broadcasted_iota(jnp.int32, a.shape, 1)
    turned = pltpu.roll(a, 4, 1)
    return jnp.where(row < 4, turned, -turned)


def circle(p):
    h = p.astype(F32) * (2.0 * math.pi / SG) - math.pi
    square = h * h
    cosine = jnp.full(h.shape, COSINE[-1], F32)
    for k in reversed(COSINE[:-1]):
        cosine = cosine * square + k
    sine = jnp.full(h.shape, SINE[-1], F32)
    for k in reversed(SINE[:-1]):
        sine = sine * square + k
    return -cosine, -sine * h


def kernel(
    plan, facet, position, u_fine, v_fine, observed, count, high, low, back,
    res_out, image_out,
    image, slots, s_a, r_a, s_p, r_p, s_b, r_b, s_c, r_c, s_d, r_d, s_e, r_e, s_f, r_f,
    wu, tch, tcl, tsh, tsl, send_sem, recv_sem,
):
    devices, nsub = plan.devices, plan.nsub
    me = lax.axis_index("facet") * nsub + lax.axis_index("sub")
    half = devices * 8

    def place(i):
        target = lax.rem(me + i, devices)
        return target, (target // nsub, lax.rem(target, nsub))

    barrier = pltpu.get_barrier_semaphore()

    def greet(i, carry):
        pl.semaphore_signal(barrier, inc=1, device_id=place(i)[1], device_id_type=MESH)
        return carry

    lax.fori_loop(1, devices, greet, 0)

    def send(phase, source, target, same=False):
        def one(i, carry):
            to, device = place(i)
            pltpu.make_async_remote_copy(
                src_ref=source if same else source.at[to],
                dst_ref=target.at[me],
                send_sem=send_sem.at[phase],
                recv_sem=recv_sem.at[phase],
                device_id=device,
                device_id_type=MESH,
            ).start()
            return carry

        lax.fori_loop(1, devices, one, 0)
        target[me] = source[...] if same else source[me]

    def wait(sem, phase, target):
        others = target.at[pl.ds(0, devices - 1)]
        pltpu.make_async_copy(others, others, sem.at[phase]).wait()

    tiles = facet.shape[2] // 128
    per = 128 // plan.xl
    for k in range(tiles):
        image[:, k] = facet[:, :, k * 128 : (k + 1) * 128].astype(F32)
    slots[...] = jnp.zeros_like(slots)
    lane = lax.broadcasted_iota(jnp.int32, (plan.vg, 128), 1)

    def rows(c, k, v, g):
        return pl.ds(g * 8 + c * 4 + k * plan.v2 + v, plan.vg, stride=plan.xg * 8)

    for c in range(2):
        for k in range(plan.rl):
            for v in range(plan.v2):
                for g in range(plan.xg):
                    tile = (k * SG + g * plan.xl) // 128
                    value = image[c, tile, pl.ds(v, plan.vg, stride=plan.v2), :]
                    if per > 1:
                        if g % per:
                            value = pltpu.roll(value, 128 - (g % per) * plan.xl, 1)
                        value = jnp.where(lane < plan.xl, value, 0.0)
                    slots[rows(c, k, v, g), :] = value
    s_a[...] = slots[...].reshape(devices, 8, 128).astype(BF16)
    s_p[...] = jnp.broadcast_to(position[...] // plan.nb, s_p.shape)

    pl.semaphore_wait(barrier, devices - 1)
    send(0, s_a, r_a)
    send(6, s_p, r_p, same=True)

    cu = u_fine[...] // OVER
    shift = (KS - 1) / 2.0 + (u_fine[...] % OVER).astype(F32) / OVER
    for i in range(plan.rl):
        row = lax.broadcasted_iota(jnp.int32, (half, u_fine.shape[1]), 0)
        cell = plan.nb * (row & 7) + (row >> 3) * plan.rl + i
        offset = cell - cu
        distance = (offset.astype(F32) - shift) / 0.6
        weight = jnp.exp(-0.5 * distance * distance)
        weight = jnp.where((offset >= 0) & (offset < KS), weight, 0.0)
        wu[pl.ds(i * half, half), :] = weight.astype(BF16)

    shape = (plan.q, v_fine.shape[1])
    row = lax.broadcasted_iota(jnp.int32, shape, 0)
    offset = (row >> 3) * plan.v2 + lax.rem(row & 3, plan.v2) - v_fine[...] // OVER
    shift = (KS - 1) / 2.0 + (v_fine[...] % OVER).astype(F32) / OVER
    distance = (offset.astype(F32) - shift) / 0.6
    wv = jnp.exp(-0.5 * distance * distance)
    wv = jnp.where((offset >= 0) & (offset < KS), wv, 0.0)

    row = lax.broadcasted_iota(jnp.int32, (8, plan.x), 0)
    lane8 = lax.broadcasted_iota(jnp.int32, (8, plan.x), 1)
    x = (lane8 >> 7) * plan.xl + (lane8 & 127)
    r = me * plan.rl + lax.div(row & 3, plan.v2)
    angle = (2.0 * math.pi / plan.width) * lax.rem(x * r, plan.width).astype(F32)
    scale = 1.0 / math.sqrt(plan.width)
    tw_c = (jnp.cos(angle) * scale)[None]
    tw_s = (jnp.sin(angle) * scale)[None]

    wait(recv_sem, 0, r_a)

    data = r_a[...].astype(F32).reshape(half, 128).astype(BF16)
    total = jnp.dot(high[...], data, preferred_element_type=F32)
    total += jnp.dot(low[...], data, preferred_element_type=F32)
    s_b[...] = total.reshape(devices, 8, 128)
    send(1, s_b, r_b)

    wait(recv_sem, 6, r_p)
    cell = (devices, 8, 128)
    m = r_p[...] + lax.broadcasted_iota(jnp.int32, cell, 1)
    in_tile = lax.broadcasted_iota(jnp.int32, cell, 2)
    for g in range(plan.xg):
        lanes = pl.ds(g * 128, 128)
        tc, ts = circle((m * (in_tile + g * plan.xl)) & (SG - 1))
        tch[:, lanes], tcl[:, lanes] = split(tc.reshape(half, 128))
        tsh[:, lanes], tsl[:, lanes] = split(ts.reshape(half, 128))

    wait(recv_sem, 1, r_b)

    got = r_b[...].reshape(plan.vg, plan.xg, 8, 128)
    a = jnp.concatenate([got[:, g] for g in range(plan.xg)], axis=2)
    a = a * tw_c + swapped(a) * tw_s
    a_h, a_l = split(a.reshape(plan.q, plan.x))
    w_h, w_l = split(swapped(a).reshape(plan.q, plan.x))
    grid = nt(tch[...], jnp.concatenate([a_h, a_l], axis=0))
    grid += nt(tsh[...], jnp.concatenate([w_h, w_l], axis=0))
    grid = grid[:, : plan.q] + grid[:, plan.q :]
    grid += nt(tcl[...], a_h) + nt(tsl[...], w_h)
    s_c[...] = grid.reshape(devices, 8, plan.q).astype(BF16)
    send(2, s_c, r_c)
    wait(recv_sem, 2, r_c)

    cells = r_c[...].astype(F32).reshape(half, plan.q)
    column = lax.broadcasted_iota(jnp.int32, (half, plan.q), 1)
    residue = lax.div(column & 3, plan.v2)
    parts = [jnp.where(residue == i, cells, 0.0) for i in range(plan.rl)]
    cells = jnp.concatenate(parts, axis=0).astype(BF16)
    along = tn(cells, wu[...]) * wv
    along = jnp.sum(along.reshape(plan.vg, 8, -1), axis=0)
    live = lax.broadcasted_iota(jnp.int32, (1, shape[1]), 1) < count[...]
    real = jnp.where(live, observed[0] - jnp.sum(along[0:4], axis=0, keepdims=True), 0.0)
    imag = jnp.where(live, observed[1] - jnp.sum(along[4:8], axis=0, keepdims=True), 0.0)
    res_out[0] = real
    res_out[1] = imag
    row = lax.broadcasted_iota(jnp.int32, shape, 0)
    spread = (wv * jnp.where((row & 7) < 4, real, imag)).astype(BF16)
    both = nt(wu[...], spread)
    regrid = both[0:half]
    for i in range(1, plan.rl):
        regrid = jnp.where(residue == i, both[i * half : (i + 1) * half], regrid)
    s_d[...] = regrid.reshape(devices, 8, plan.q).astype(BF16)
    send(3, s_d, r_d)
    wait(recv_sem, 3, r_d)

    cells = r_d[...].astype(F32).reshape(half, plan.q).astype(BF16)
    first = tn(cells, tch[...]).reshape(plan.vg, 8, plan.x)
    second = tn(cells, tsh[...]).reshape(plan.vg, 8, plan.x)
    a = first - swapped(second)
    a = a * tw_c - swapped(a) * tw_s
    parts = [a[:, None, :, g * 128 : (g + 1) * 128] for g in range(plan.xg)]
    s_e[...] = jnp.concatenate(parts, axis=1).reshape(devices, 8, 128).astype(BF16)
    send(4, s_e, r_e)
    wait(recv_sem, 4, r_e)

    data = r_e[...].astype(F32).reshape(half, 128).astype(BF16)
    total = jnp.dot(back[...], data, preferred_element_type=F32)
    s_f[...] = total.reshape(devices, 8, 128).astype(BF16)
    send(5, s_f, r_f)
    wait(recv_sem, 5, r_f)

    slots[...] = r_f[...].astype(F32).reshape(half, 128)
    for c in range(2):
        for k in range(plan.rl):
            for v in range(plan.v2):
                for g in range(0, plan.xg, per):
                    value = slots[rows(c, k, v, g), :]
                    for n in range(1, per):
                        more = pltpu.roll(slots[rows(c, k, v, g + n), :], n * plan.xl, 1)
                        value = jnp.where(lane < n * plan.xl, value, more)
                    tile = (k * SG + g * plan.xl) // 128
                    image[c, tile, pl.ds(v, plan.vg, stride=plan.v2), :] = value
    for k in range(tiles):
        image_out[:, :, k * 128 : (k + 1) * 128] = image[:, k]

    for phase, sent in enumerate((r_a, r_b, r_c, r_d, r_e, r_f, r_p)):
        wait(send_sem, phase, sent)


def shards(facet_data, subgrid_pos, vis_counts, vis_u_fine, vis_v_fine, vis_observed):
    nsub = lax.axis_size("sub")
    devices = lax.axis_size("facet") * nsub
    plan = Plan(devices, nsub, facet_data.shape[1], facet_data.shape[2])
    slots = vis_u_fine.shape[1]

    table = block_transform(plan)
    high = table.astype(BF16)
    low = (table - high.astype(np.float32)).astype(BF16)

    wide = pltpu.VMEM((devices, 8, 128), F32)
    tile = pltpu.VMEM((devices, 8, 128), BF16)
    cell = pltpu.VMEM((devices, 8, plan.q), BF16)
    turn = pltpu.VMEM((devices * 8, plan.x), BF16)
    rows_v, columns = facet_data.shape[1:]
    return pl.pallas_call(
        functools.partial(kernel, plan),
        out_shape=(
            jax.ShapeDtypeStruct(vis_observed.shape, F32),
            jax.ShapeDtypeStruct(facet_data.shape, F32),
        ),
        in_specs=[pl.BlockSpec(memory_space=pltpu.VMEM)] * 9,
        out_specs=(pl.BlockSpec(memory_space=pltpu.VMEM),) * 2,
        scratch_shapes=[
            pltpu.VMEM((2, columns // 128, rows_v, 128), F32),
            pltpu.VMEM((devices * 8, 128), F32),
            tile, tile,
            pltpu.VMEM((1, 128), jnp.int32),
            pltpu.VMEM((devices, 1, 128), jnp.int32),
            wide, wide, cell, cell, cell, cell, tile, tile, tile, tile,
            pltpu.VMEM((plan.rl * devices * 8, slots), BF16),
            turn, turn, turn, turn,
            pltpu.SemaphoreType.DMA((7,)),
            pltpu.SemaphoreType.DMA((7,)),
        ],
        compiler_params=pltpu.CompilerParams(
            collective_id=0, has_side_effects=True, vmem_limit_bytes=48 * 1024 * 1024
        ),
    )(
        facet_data, subgrid_pos.reshape(1, 1), vis_u_fine, vis_v_fine, vis_observed,
        vis_counts.reshape(1, 1), jnp.asarray(high), jnp.asarray(low), jnp.asarray(high.T),
    )


def solution(mesh):
    return jax.shard_map(
        shards,
        mesh=mesh,
        in_specs=(
            P(None, None, ("facet", "sub")),
            P(("facet", "sub")),
            P(("facet", "sub")),
            P(("facet", "sub"), None),
            P(("facet", "sub"), None),
            P(None, ("facet", "sub"), None),
        ),
        out_specs=(P(None, ("facet", "sub"), None), P(None, None, ("facet", "sub"))),
        check_vma=False,
    )
```

time: 49.9 us -> 45.5 us (0.912)
  Pallas kernels: 44.5 us -> 37.7 us
  local copies, waits for them, and re-layouts: 2.93 us -> 5.49 us
    pallas_call x1, Pallas kernels: 44.5 us -> 37.7 us  [shards(): pl.pallas_call(functools.partial(kernel, plan), out_shape=(jax.ShapeDtype...]
    unnamed x20 -> x16, local copies, waits for them, and re-layouts: 2.04 us -> 5.49 us
    reshape x3 -> x0, local copies, waits for them, and re-layouts: 0.84 us -> none  [the longest x1 0.71 us: shards(): out = out.transpose(2, 0, 4, 3, 1, 5).reshape(facet_data.shape)]
where the time goes in v2:
time: 45.5 us; the launch traced here: 45.2 us
  Pallas kernels  37.7 us (83%)
  local copies, waits for them, and re-layouts  5.49 us (12%)
  between operations  2 us (4%)
    pallas_call x1, Pallas kernels, shards(): pl.pallas_call(functools.partial(kernel, plan), out_shape=(jax.ShapeDtype...  37.7 us
    unnamed x16, local copies, waits for them, and re-layouts  5.49 us

profile of v2, /device:TPU:0, one launch (start us, length us, event | category | flops | bytes accessed | tf_op | source)
XLA Modules:
  0.0 45.2 jit_solution(12958263714194326569)
XLA Ops:
  0.6 0.0 copy-start.4
  1.3 0.0 copy-start.5
  2.0 0.0 copy-done.4
  2.0 0.0 copy-done.5
  2.0 0.0 copy-start
  2.0 0.9 %copy-done = bf16[256,256]{1,0:T(8,128)(2,1)S(1)} copy-done((bf16[256,256]{1,0:T(8,128)(2,1)S(1)}, bf16[256,256]{1,0:T(8,128)(2,1)}, u32[]{:S(2)}) %copy-start) | copy-done | bytes 131096
  2.9 0.0 copy-start.1
  2.9 0.9 %copy-done.1 = bf16[256,256]{1,0:T(8,128)(2,1)S(1)} copy-done((bf16[256,256]{1,0:T(8,128)(2,1)S(1)}, bf16[256,256]{1,0:T(8,128)(2,1)}, u32[]{:S(2)}) %copy-start.1) | copy-done | bytes 131096
  3.8 0.0 copy-start.2
  3.8 0.9 %copy-done.2 = bf16[256,256]{1,0:T(8,128)(2,1)S(1)} copy-done((bf16[256,256]{1,0:T(8,128)(2,1)S(1)}, bf16[256,256]{1,0:T(8,128)(2,1)}, u32[]{:S(2)}) %copy-start.2) | copy-done | bytes 131096
  4.7 0.0 copy-start.3
  4.7 0.8 %copy-done.3 = bf16[2,16,1024]{2,1,0:T(8,128)(2,1)S(1)} copy-done((bf16[2,16,1024]{2,1,0:T(8,128)(2,1)S(1)}, bf16[2,16,1024]{2,1,0:T(8,128)(2,1)}, u32[]{:S(2)}) %copy-start.3) | copy-done | bytes 65560
  5.5 0.0 copy-start.6
  5.5 0.7 %copy-done.6 = s32[1,512]{1,0:T(1,128)S(1)} copy-done((s32[1,512]{1,0:T(1,128)S(1)}, s32[1,512]{1,0:T(1,128)}, u32[]{:S(2)}) %copy-start.6) | copy-done | bytes 2072
  6.2 37.7 %shard_map.104 = (f32[2,1,512]{2,1,0:T(1,128)S(1)}, f32[2,16,1024]{2,1,0:T(8,128)S(1)}) custom-call(bf16[2,16,1024]{2,1,0:T(8,128)(2,1)S(1)} %copy-done.3, s32[1,1]{1,0:T(1,128)} %bitcast.2.position, s32[1,512]{1,0:T(1,128)S(1)} %copy-done.5, s32[1,512]{1,0:T(1,128)S(1)} %copy-done.6, f32[2,1,512]{2,1,0:T(1,128)S(1)} %copy-done.4, s32[1,1]{1,0:T(1,128)} %bitcast.3.count, ...), custom_call_target="tpu_custom_call" | custom-call | tf_op jit(solution)/shard_map/pallas_call | solution.py:290
  44.0 0.6 %copy.15 = f32[2,1,512]{2,1,0:T(1,128)} copy(f32[2,1,512]{2,1,0:T(1,128)S(1)} %get-tuple-element.4) | data formatting | bytes 8192
  44.6 0.7 %copy.16 = f32[2,16,1024]{2,1,0:T(8,128)} copy(f32[2,16,1024]{2,1,0:T(8,128)S(1)} %get-tuple-element.5) | data formatting | bytes 262144
Async XLA Ops:
  0.6 1.3 %copy-start.4 = (f32[2,1,512]{2,1,0:T(1,128)S(1)}, f32[2,1,512]{2,1,0:T(1,128)}, u32[]{:S(2)}) copy-start(f32[2,1,512]{2,1,0:T(1,128)} %observed.1) | copy-start | bytes 12292
  1.3 0.7 %copy-start.5 = (s32[1,512]{1,0:T(1,128)S(1)}, s32[1,512]{1,0:T(1,128)}, u32[]{:S(2)}) copy-start(s32[1,512]{1,0:T(1,128)} %u_fine.1) | copy-start | bytes 6148
  2.0 0.9 %copy-start = (bf16[256,256]{1,0:T(8,128)(2,1)S(1)}, bf16[256,256]{1,0:T(8,128)(2,1)}, u32[]{:S(2)}) copy-start(bf16[256,256]{1,0:T(8,128)(2,1)} %constant.8.clone.back) | copy-start | bytes 393220
  2.9 0.9 %copy-start.1 = (bf16[256,256]{1,0:T(8,128)(2,1)S(1)}, bf16[256,256]{1,0:T(8,128)(2,1)}, u32[]{:S(2)}) copy-start(bf16[256,256]{1,0:T(8,128)(2,1)} %constant.7.clone.low) | copy-start | bytes 393220
  3.8 0.9 %copy-start.2 = (bf16[256,256]{1,0:T(8,128)(2,1)S(1)}, bf16[256,256]{1,0:T(8,128)(2,1)}, u32[]{:S(2)}) copy-start(bf16[256,256]{1,0:T(8,128)(2,1)} %constant.6.clone.high) | copy-start | bytes 393220
  4.7 0.8 %copy-start.3 = (bf16[2,16,1024]{2,1,0:T(8,128)(2,1)S(1)}, bf16[2,16,1024]{2,1,0:T(8,128)(2,1)}, u32[]{:S(2)}) copy-start(bf16[2,16,1024]{2,1,0:T(8,128)(2,1)} %facet.1) | copy-start | bytes 196612
  5.5 0.7 %copy-start.6 = (s32[1,512]{1,0:T(1,128)S(1)}, s32[1,512]{1,0:T(1,128)}, u32[]{:S(2)}) copy-start(s32[1,512]{1,0:T(1,128)} %v_fine.1) | copy-start | bytes 6148

commit v3 on v2

--- a/solution.py
+++ b/solution.py
@@ -35,6 +35,7 @@
         self.used = self.rl * self.v2
         self.q = self.vg * 8
         self.x = self.xg * 128
+        self.partners = sorted(range(1, devices), key=lambda i: -(i % nsub))
 
 
 def block_transform(plan):
@@ -85,30 +86,35 @@
     return -cosine, -sine * h
 
 
-def kernel(
-    plan, facet, position, u_fine, v_fine, observed, count, high, low, back,
-    res_out, image_out,
-    image, slots, s_a, r_a, s_p, r_p, s_b, r_b, s_c, r_c, s_d, r_d, s_e, r_e, s_f, r_f,
-    wu, tch, tcl, tsh, tsl, send_sem, recv_sem,
-):
+def kernel(plan, *refs):
+    operands, (res_out, image_out) = refs[:9], refs[9:11]
+    (
+        image, slots, s_a, r_a, s_p, r_p, s_b, r_b, s_c, r_c, s_d, r_d, s_e, r_e, s_f, r_f,
+        wu, tch, tcl, tsh, tsl, send_sem, recv_sem, load_sem,
+    ) = refs[11:35]
+    held = refs[35:]
+    facet, position, u_fine, v_fine, observed, count, high, low, back = held
     devices, nsub = plan.devices, plan.nsub
     me = lax.axis_index("facet") * nsub + lax.axis_index("sub")
     half = devices * 8
 
+    loads = [
+        pltpu.make_async_copy(operand, own, load_sem.at[n])
+        for n, (operand, own) in enumerate(zip(operands, held))
+    ]
+    for load in loads:
+        load.start()
+
     def place(i):
-        target = lax.rem(me + i, devices)
+        target = me ^ i
         return target, (target // nsub, lax.rem(target, nsub))
 
     barrier = pltpu.get_barrier_semaphore()
-
-    def greet(i, carry):
+    for i in plan.partners:
         pl.semaphore_signal(barrier, inc=1, device_id=place(i)[1], device_id_type=MESH)
-        return carry
-
-    lax.fori_loop(1, devices, greet, 0)
 
     def send(phase, source, target, same=False):
-        def one(i, carry):
+        for i in plan.partners:
             to, device = place(i)
             pltpu.make_async_remote_copy(
                 src_ref=source if same else source.at[to],
@@ -118,15 +124,14 @@
                 device_id=device,
                 device_id_type=MESH,
             ).start()
-            return carry
-
-        lax.fori_loop(1, devices, one, 0)
         target[me] = source[...] if same else source[me]
 
     def wait(sem, phase, target):
         others = target.at[pl.ds(0, devices - 1)]
         pltpu.make_async_copy(others, others, sem.at[phase]).wait()
 
+    loads[0].wait()
+    loads[1].wait()
     tiles = facet.shape[2] // 128
     per = 128 // plan.xl
     for k in range(tiles):
@@ -155,6 +160,7 @@
     send(0, s_a, r_a)
     send(6, s_p, r_p, same=True)
 
+    loads[2].wait()
     cu = u_fine[...] // OVER
     shift = (KS - 1) / 2.0 + (u_fine[...] % OVER).astype(F32) / OVER
     for i in range(plan.rl):
@@ -166,6 +172,7 @@
         weight = jnp.where((offset >= 0) & (offset < KS), weight, 0.0)
         wu[pl.ds(i * half, half), :] = weight.astype(BF16)
 
+    loads[3].wait()
     shape = (plan.q, v_fine.shape[1])
     row = lax.broadcasted_iota(jnp.int32, shape, 0)
     offset = (row >> 3) * plan.v2 + lax.rem(row & 3, plan.v2) - v_fine[...] // OVER
@@ -183,6 +190,8 @@
     tw_c = (jnp.cos(angle) * scale)[None]
     tw_s = (jnp.sin(angle) * scale)[None]
 
+    for load in loads[4:]:
+        load.wait()
     wait(recv_sem, 0, r_a)
 
     data = r_a[...].astype(F32).reshape(half, 128).astype(BF16)
@@ -287,13 +296,17 @@
     cell = pltpu.VMEM((devices, 8, plan.q), BF16)
     turn = pltpu.VMEM((devices * 8, plan.x), BF16)
     rows_v, columns = facet_data.shape[1:]
+    operands = (
+        facet_data, subgrid_pos.reshape(1, 1), vis_u_fine, vis_v_fine, vis_observed,
+        vis_counts.reshape(1, 1), jnp.asarray(high), jnp.asarray(low), jnp.asarray(high.T),
+    )
     return pl.pallas_call(
         functools.partial(kernel, plan),
         out_shape=(
             jax.ShapeDtypeStruct(vis_observed.shape, F32),
             jax.ShapeDtypeStruct(facet_data.shape, F32),
         ),
-        in_specs=[pl.BlockSpec(memory_space=pltpu.VMEM)] * 9,
+        in_specs=[pl.BlockSpec(memory_space=pltpu.HBM)] * 9,
         out_specs=(pl.BlockSpec(memory_space=pltpu.VMEM),) * 2,
         scratch_shapes=[
             pltpu.VMEM((2, columns // 128, rows_v, 128), F32),
@@ -306,14 +319,13 @@
             turn, turn, turn, turn,
             pltpu.SemaphoreType.DMA((7,)),
             pltpu.SemaphoreType.DMA((7,)),
-        ],
+            pltpu.SemaphoreType.DMA((9,)),
+        ]
+        + [pltpu.VMEM(one.shape, one.dtype) for one in operands],
         compiler_params=pltpu.CompilerParams(
-            collective_id=0, has_side_effects=True, vmem_limit_bytes=48 * 1024 * 1024
+            collective_id=0, has_side_effects=True, vmem_limit_bytes=64 * 1024 * 1024 - 65536
         ),
-    )(
-        facet_data, subgrid_pos.reshape(1, 1), vis_u_fine, vis_v_fine, vis_observed,
-        vis_counts.reshape(1, 1), jnp.asarray(high), jnp.asarray(low), jnp.asarray(high.T),
-    )
+    )(*operands)
 
 
 def solution(mesh):

time: 45.5 us -> 42.7 us (0.938)
  local copies, waits for them, and re-layouts: 5.49 us -> 2.85 us
    unnamed x16 -> x2, local copies, waits for them, and re-layouts: 5.49 us -> 2.85 us
where the time goes in v3:
time: 42.7 us; the launch traced here: 42.5 us
  Pallas kernels  37.7 us (88%)
  local copies, waits for them, and re-layouts  2.85 us (7%)
  between operations  1.93 us (5%)
    pallas_call x1, Pallas kernels, shards(): pl.pallas_call(functools.partial(kernel, plan), out_shape=(jax.ShapeDtype...  37.7 us
    unnamed x2, local copies, waits for them, and re-layouts  2.85 us

profile of v3, /device:TPU:0, one launch (start us, length us, event | category | flops | bytes accessed | tf_op | source)
XLA Modules:
  0.0 42.5 jit_solution(4406876802619280810)
XLA Ops:
  1.9 37.7 %shard_map.104 = (f32[2,1,512]{2,1,0:T(1,128)}, f32[2,16,1024]{2,1,0:T(8,128)}) custom-call(bf16[2,16,1024]{2,1,0:T(8,128)(2,1)} %refs_0_.1, s32[1,1]{1,0:T(1,128)} %bitcast.2.refs_1_, s32[1,512]{1,0:T(1,128)} %refs_2_.1, s32[1,512]{1,0:T(1,128)} %refs_3_.1, f32[2,1,512]{2,1,0:T(1,128)} %refs_4_.1, s32[1,1]{1,0:T(1,128)} %bitcast.3.refs_5_, ...), custom_call_target="tpu_custom_call" | custom-call | tf_op jit(solution)/shard_map/pallas_call | solution.py:303
  39.7 1.3 %copy.15 = f32[2,1,512]{2,1,0:T(1,128)} copy(f32[2,1,512]{2,1,0:T(1,128)} %get-tuple-element.4) | data formatting | bytes 8192
  40.9 1.6 %copy.16 = f32[2,16,1024]{2,1,0:T(8,128)} copy(f32[2,16,1024]{2,1,0:T(8,128)} %get-tuple-element.5) | data formatting | bytes 262144

commit v4 on v3

--- a/solution.py
+++ b/solution.py
@@ -86,11 +86,15 @@
     return -cosine, -sine * h
 
 
+def rows(plan, c, k, v, g):
+    return pl.ds(g * 8 + c * 4 + k * plan.v2 + v, plan.vg, stride=plan.xg * 8)
+
+
 def kernel(plan, *refs):
-    operands, (res_out, image_out) = refs[:9], refs[9:11]
+    operands, (res_out, r_f) = refs[:9], refs[9:11]
     (
-        image, slots, s_a, r_a, s_p, r_p, s_b, r_b, s_c, r_c, s_d, r_d, s_e, r_e, s_f, r_f,
-        wu, tch, tcl, tsh, tsl, send_sem, recv_sem, load_sem,
+        image, slots, s_a, r_a, s_p, r_p, s_b, r_b, s_c, r_c, s_d, r_d, s_e, r_e, s_f,
+        res, wu, tch, tcl, tsh, tsl, send_sem, recv_sem, load_sem,
     ) = refs[11:35]
     held = refs[35:]
     facet, position, u_fine, v_fine, observed, count, high, low, back = held
@@ -113,7 +117,7 @@
     for i in plan.partners:
         pl.semaphore_signal(barrier, inc=1, device_id=place(i)[1], device_id_type=MESH)
 
-    def send(phase, source, target, same=False):
+    def send(phase, source, target, same=False, local=False):
         for i in plan.partners:
             to, device = place(i)
             pltpu.make_async_remote_copy(
@@ -124,7 +128,8 @@
                 device_id=device,
                 device_id_type=MESH,
             ).start()
-        target[me] = source[...] if same else source[me]
+        if not local:
+            target[me] = source[...] if same else source[me]
 
     def wait(sem, phase, target):
         others = target.at[pl.ds(0, devices - 1)]
@@ -138,9 +143,6 @@
         image[:, k] = facet[:, :, k * 128 : (k + 1) * 128].astype(F32)
     slots[...] = jnp.zeros_like(slots)
     lane = lax.broadcasted_iota(jnp.int32, (plan.vg, 128), 1)
-
-    def rows(c, k, v, g):
-        return pl.ds(g * 8 + c * 4 + k * plan.v2 + v, plan.vg, stride=plan.xg * 8)
 
     for c in range(2):
         for k in range(plan.rl):
@@ -152,34 +154,13 @@
                         if g % per:
                             value = pltpu.roll(value, 128 - (g % per) * plan.xl, 1)
                         value = jnp.where(lane < plan.xl, value, 0.0)
-                    slots[rows(c, k, v, g), :] = value
+                    slots[rows(plan, c, k, v, g), :] = value
     s_a[...] = slots[...].reshape(devices, 8, 128).astype(BF16)
     s_p[...] = jnp.broadcast_to(position[...] // plan.nb, s_p.shape)
 
     pl.semaphore_wait(barrier, devices - 1)
     send(0, s_a, r_a)
     send(6, s_p, r_p, same=True)
-
-    loads[2].wait()
-    cu = u_fine[...] // OVER
-    shift = (KS - 1) / 2.0 + (u_fine[...] % OVER).astype(F32) / OVER
-    for i in range(plan.rl):
-        row = lax.broadcasted_iota(jnp.int32, (half, u_fine.shape[1]), 0)
-        cell = plan.nb * (row & 7) + (row >> 3) * plan.rl + i
-        offset = cell - cu
-        distance = (offset.astype(F32) - shift) / 0.6
-        weight = jnp.exp(-0.5 * distance * distance)
-        weight = jnp.where((offset >= 0) & (offset < KS), weight, 0.0)
-        wu[pl.ds(i * half, half), :] = weight.astype(BF16)
-
-    loads[3].wait()
-    shape = (plan.q, v_fine.shape[1])
-    row = lax.broadcasted_iota(jnp.int32, shape, 0)
-    offset = (row >> 3) * plan.v2 + lax.rem(row & 3, plan.v2) - v_fine[...] // OVER
-    shift = (KS - 1) / 2.0 + (v_fine[...] % OVER).astype(F32) / OVER
-    distance = (offset.astype(F32) - shift) / 0.6
-    wv = jnp.exp(-0.5 * distance * distance)
-    wv = jnp.where((offset >= 0) & (offset < KS), wv, 0.0)
 
     row = lax.broadcasted_iota(jnp.int32, (8, plan.x), 0)
     lane8 = lax.broadcasted_iota(jnp.int32, (8, plan.x), 1)
@@ -190,7 +171,7 @@
     tw_c = (jnp.cos(angle) * scale)[None]
     tw_s = (jnp.sin(angle) * scale)[None]
 
-    for load in loads[4:]:
+    for load in loads[2:]:
         load.wait()
     wait(recv_sem, 0, r_a)
 
@@ -223,6 +204,26 @@
     grid += nt(tcl[...], a_h) + nt(tsl[...], w_h)
     s_c[...] = grid.reshape(devices, 8, plan.q).astype(BF16)
     send(2, s_c, r_c)
+
+    cu = u_fine[...] // OVER
+    shift = (KS - 1) / 2.0 + (u_fine[...] % OVER).astype(F32) / OVER
+    for i in range(plan.rl):
+        row = lax.broadcasted_iota(jnp.int32, (half, u_fine.shape[1]), 0)
+        cell = plan.nb * (row & 7) + (row >> 3) * plan.rl + i
+        offset = cell - cu
+        distance = (offset.astype(F32) - shift) / 0.6
+        weight = jnp.exp(-0.5 * distance * distance)
+        weight = jnp.where((offset >= 0) & (offset < KS), weight, 0.0)
+        wu[pl.ds(i * half, half), :] = weight.astype(BF16)
+
+    shape = (plan.q, v_fine.shape[1])
+    row = lax.broadcasted_iota(jnp.int32, shape, 0)
+    offset = (row >> 3) * plan.v2 + lax.rem(row & 3, plan.v2) - v_fine[...] // OVER
+    shift = (KS - 1) / 2.0 + (v_fine[...] % OVER).astype(F32) / OVER
+    distance = (offset.astype(F32) - shift) / 0.6
+    wv = jnp.exp(-0.5 * distance * distance)
+    wv = jnp.where((offset >= 0) & (offset < KS), wv, 0.0)
+
     wait(recv_sem, 2, r_c)
 
     cells = r_c[...].astype(F32).reshape(half, plan.q)
@@ -235,8 +236,10 @@
     live = lax.broadcasted_iota(jnp.int32, (1, shape[1]), 1) < count[...]
     real = jnp.where(live, observed[0] - jnp.sum(along[0:4], axis=0, keepdims=True), 0.0)
     imag = jnp.where(live, observed[1] - jnp.sum(along[4:8], axis=0, keepdims=True), 0.0)
-    res_out[0] = real
-    res_out[1] = imag
+    res[0] = real
+    res[1] = imag
+    kept = pltpu.make_async_copy(res, res_out, load_sem.at[0])
+    kept.start()
     row = lax.broadcasted_iota(jnp.int32, shape, 0)
     spread = (wv * jnp.where((row & 7) < 4, real, imag)).astype(BF16)
     both = nt(wu[...], spread)
@@ -260,25 +263,35 @@
     data = r_e[...].astype(F32).reshape(half, 128).astype(BF16)
     total = jnp.dot(back[...], data, preferred_element_type=F32)
     s_f[...] = total.reshape(devices, 8, 128).astype(BF16)
-    send(5, s_f, r_f)
+    send(5, s_f, r_f, local=True)
+    own = pltpu.make_async_copy(s_f.at[me], r_f.at[me], load_sem.at[1])
+    own.start()
     wait(recv_sem, 5, r_f)
-
-    slots[...] = r_f[...].astype(F32).reshape(half, 128)
+    own.wait()
+    kept.wait()
+
+    for phase, sent in enumerate((r_a, r_b, r_c, r_d, r_e, r_f, r_p)):
+        wait(send_sem, phase, sent)
+
+
+def finish(plan, residual, got, res_out, image_out, image, slots):
+    res_out[...] = residual[...]
+    tiles = image_out.shape[2] // 128
+    per = 128 // plan.xl
+    lane = lax.broadcasted_iota(jnp.int32, (plan.vg, 128), 1)
+    slots[...] = got[...].astype(F32).reshape(plan.devices * 8, 128)
     for c in range(2):
         for k in range(plan.rl):
             for v in range(plan.v2):
                 for g in range(0, plan.xg, per):
-                    value = slots[rows(c, k, v, g), :]
+                    value = slots[rows(plan, c, k, v, g), :]
                     for n in range(1, per):
-                        more = pltpu.roll(slots[rows(c, k, v, g + n), :], n * plan.xl, 1)
+                        more = pltpu.roll(slots[rows(plan, c, k, v, g + n), :], n * plan.xl, 1)
                         value = jnp.where(lane < n * plan.xl, value, more)
                     tile = (k * SG + g * plan.xl) // 128
                     image[c, tile, pl.ds(v, plan.vg, stride=plan.v2), :] = value
     for k in range(tiles):
         image_out[:, :, k * 128 : (k + 1) * 128] = image[:, k]
-
-    for phase, sent in enumerate((r_a, r_b, r_c, r_d, r_e, r_f, r_p)):
-        wait(send_sem, phase, sent)
 
 
 def shards(facet_data, subgrid_pos, vis_counts, vis_u_fine, vis_v_fine, vis_observed):
@@ -300,21 +313,22 @@
         facet_data, subgrid_pos.reshape(1, 1), vis_u_fine, vis_v_fine, vis_observed,
         vis_counts.reshape(1, 1), jnp.asarray(high), jnp.asarray(low), jnp.asarray(high.T),
     )
-    return pl.pallas_call(
+    residual, got = pl.pallas_call(
         functools.partial(kernel, plan),
         out_shape=(
             jax.ShapeDtypeStruct(vis_observed.shape, F32),
-            jax.ShapeDtypeStruct(facet_data.shape, F32),
+            jax.ShapeDtypeStruct((devices, 8, 128), BF16),
         ),
         in_specs=[pl.BlockSpec(memory_space=pltpu.HBM)] * 9,
-        out_specs=(pl.BlockSpec(memory_space=pltpu.VMEM),) * 2,
+        out_specs=(pl.BlockSpec(memory_space=pltpu.HBM),) * 2,
         scratch_shapes=[
             pltpu.VMEM((2, columns // 128, rows_v, 128), F32),
             pltpu.VMEM((devices * 8, 128), F32),
             tile, tile,
             pltpu.VMEM((1, 128), jnp.int32),
             pltpu.VMEM((devices, 1, 128), jnp.int32),
-            wide, wide, cell, cell, cell, cell, tile, tile, tile, tile,
+            wide, wide, cell, cell, cell, cell, tile, tile, tile,
+            pltpu.VMEM(vis_observed.shape, F32),
             pltpu.VMEM((plan.rl * devices * 8, slots), BF16),
             turn, turn, turn, turn,
             pltpu.SemaphoreType.DMA((7,)),
@@ -326,6 +340,20 @@
             collective_id=0, has_side_effects=True, vmem_limit_bytes=64 * 1024 * 1024 - 65536
         ),
     )(*operands)
+    return pl.pallas_call(
+        functools.partial(finish, plan),
+        out_shape=(
+            jax.ShapeDtypeStruct(vis_observed.shape, F32),
+            jax.ShapeDtypeStruct(facet_data.shape, F32),
+        ),
+        in_specs=[pl.BlockSpec(memory_space=pltpu.VMEM)] * 2,
+        out_specs=(pl.BlockSpec(memory_space=pltpu.VMEM),) * 2,
+        scratch_shapes=[
+            pltpu.VMEM((2, columns // 128, rows_v, 128), F32),
+            pltpu.VMEM((devices * 8, 128), F32),
+        ],
+        compiler_params=pltpu.CompilerParams(vmem_limit_bytes=64 * 1024 * 1024 - 65536),
+    )(residual, got)
 
 
 def solution(mesh):

time: 42.7 us -> 40.8 us (0.956)
  local copies, waits for them, and re-layouts: 2.85 us -> 0 us
  Pallas kernels: 37.7 us -> 38.7 us
    unnamed x2 -> x0, local copies, waits for them, and re-layouts: 2.85 us -> none
    pallas_call x0 -> x1, Pallas kernels: none -> 1.6 us  [shards(): pl.pallas_call(functools.partial(finish, plan), out_shape=(jax.ShapeDtype...]
    pallas_call x1, Pallas kernels: 37.7 us -> 37.1 us  [shards(): pl.pallas_call(functools.partial(kernel, plan), out_shape=(jax.ShapeDtype...]
where the time goes in v4:
time: 40.8 us; the launch traced here: 40.6 us
  Pallas kernels  38.7 us (95%)
  between operations  1.93 us (5%)
    pallas_call x1, Pallas kernels, shards(): pl.pallas_call(functools.partial(kernel, plan), out_shape=(jax.ShapeDtype...  37.1 us
    pallas_call x1, Pallas kernels, shards(): pl.pallas_call(functools.partial(finish, plan), out_shape=(jax.ShapeDtype...  1.6 us

profile of v4, /device:TPU:0, one launch (start us, length us, event | category | flops | bytes accessed | tf_op | source)
XLA Modules:
  0.0 40.6 jit_solution(17099394530990205126)
XLA Ops:
  1.9 37.1 %shard_map.104 = (f32[2,1,512]{2,1,0:T(1,128)}, bf16[32,8,128]{2,1,0:T(8,128)(2,1)}) custom-call(bf16[2,16,1024]{2,1,0:T(8,128)(2,1)} %refs_0_.1, s32[1,1]{1,0:T(1,128)} %bitcast.2.refs_1_, s32[1,512]{1,0:T(1,128)} %refs_2_.1, s32[1,512]{1,0:T(1,128)} %refs_3_.1, f32[2,1,512]{2,1,0:T(1,128)} %refs_4_.1, s32[1,1]{1,0:T(1,128)} %bitcast.3.refs_5_, ...), custom_call_target="tpu_custom_call" | custom-call | tf_op jit(solution)/shard_map/pallas_call | solution.py:316
  39.0 1.6 %shard_map.105 = (f32[2,1,512]{2,1,0:T(1,128)}, f32[2,16,1024]{2,1,0:T(8,128)}) custom-call(f32[2,1,512]{2,1,0:T(1,128)} %get-tuple-element.4.residual, bf16[32,8,128]{2,1,0:T(8,128)(2,1)} %get-tuple-element.5.got), custom_call_target="tpu_custom_call" | custom-call | tf_op jit(solution)/shard_map/pallas_call | solution.py:343

commit v5 on v4

--- a/solution.py
+++ b/solution.py
@@ -27,13 +27,13 @@
         self.width = columns * devices
         self.nb = self.width // SG
         self.rl = self.nb // devices
-        self.times = SG // self.nb
-        self.vg = min(rows_v, devices // 4)
-        self.xg = devices // self.vg
+        self.vg = nsub
+        self.xg = devices // nsub
         self.v2 = rows_v // self.vg
         self.xl = SG // self.xg
-        self.used = self.rl * self.v2
-        self.q = self.vg * 8
+        self.res = self.nb // self.xg
+        self.cv = 2 * self.v2
+        self.q = self.cv * self.res
         self.x = self.xg * 128
         self.partners = sorted(range(1, devices), key=lambda i: -(i % nsub))
 
@@ -41,18 +41,17 @@
 def block_transform(plan):
     ids = np.arange(plan.nb)
     angle = 2.0 * np.pi * ((ids[:, None] * ids[None, :]) % plan.nb) / plan.nb
-    cosine = np.cos(angle).reshape(plan.devices, plan.rl, plan.devices, plan.rl)
-    sine = np.sin(angle).reshape(plan.devices, plan.rl, plan.devices, plan.rl)
-    table = np.zeros((plan.devices, 2, 4, plan.devices, 2, 4), np.float32)
-    for i in range(plan.rl):
-        for k in range(plan.rl):
-            for v in range(plan.v2):
-                out, into = i * plan.v2 + v, k * plan.v2 + v
-                table[:, 0, out, :, 0, into] = cosine[:, i, :, k]
-                table[:, 0, out, :, 1, into] = sine[:, i, :, k]
-                table[:, 1, out, :, 0, into] = -sine[:, i, :, k]
-                table[:, 1, out, :, 1, into] = cosine[:, i, :, k]
-    return table.reshape(plan.devices * 8, plan.devices * 8)
+    cosine = np.cos(angle).reshape(plan.xg, plan.res, plan.devices, plan.rl)
+    sine = np.sin(angle).reshape(plan.xg, plan.res, plan.devices, plan.rl)
+    table = np.zeros((plan.xg, 2, plan.v2, plan.res, plan.devices, 2, 4), np.float32)
+    for k in range(plan.rl):
+        for v in range(plan.v2):
+            into = k * plan.v2 + v
+            table[:, 0, v, :, :, 0, into] = cosine[..., k]
+            table[:, 0, v, :, :, 1, into] = sine[..., k]
+            table[:, 1, v, :, :, 0, into] = -sine[..., k]
+            table[:, 1, v, :, :, 1, into] = cosine[..., k]
+    return table.reshape(plan.xg * plan.q, plan.devices * 8)
 
 
 def nt(a, b):
@@ -69,13 +68,12 @@
 
 
 def swapped(a):
-    row = lax.broadcasted_iota(jnp.int32, a.shape, 1)
-    turned = pltpu.roll(a, 4, 1)
-    return jnp.where(row < 4, turned, -turned)
-
-
-def circle(p):
-    h = p.astype(F32) * (2.0 * math.pi / SG) - math.pi
+    middle = a.shape[0] // 2
+    return jnp.concatenate([a[middle:], -a[:middle]], axis=0)
+
+
+def circle(p, period):
+    h = p.astype(F32) * (2.0 * math.pi / period) - math.pi
     square = h * h
     cosine = jnp.full(h.shape, COSINE[-1], F32)
     for k in reversed(COSINE[:-1]):
@@ -87,7 +85,7 @@
 
 
 def rows(plan, c, k, v, g):
-    return pl.ds(g * 8 + c * 4 + k * plan.v2 + v, plan.vg, stride=plan.xg * 8)
+    return pl.ds(g * plan.vg * 8 + c * 4 + k * plan.v2 + v, plan.vg, stride=8)
 
 
 def kernel(plan, *refs):
@@ -99,7 +97,8 @@
     held = refs[35:]
     facet, position, u_fine, v_fine, observed, count, high, low, back = held
     devices, nsub = plan.devices, plan.nsub
-    me = lax.axis_index("facet") * nsub + lax.axis_index("sub")
+    group, column = lax.axis_index("facet"), lax.axis_index("sub")
+    me = group * nsub + column
     half = devices * 8
 
     loads = [
@@ -131,8 +130,20 @@
         if not local:
             target[me] = source[...] if same else source[me]
 
+    def across(phase, source, target):
+        for i in range(1, plan.xg):
+            pltpu.make_async_remote_copy(
+                src_ref=source.at[group ^ i],
+                dst_ref=target.at[group],
+                send_sem=send_sem.at[phase],
+                recv_sem=recv_sem.at[phase],
+                device_id=(group ^ i, column),
+                device_id_type=MESH,
+            ).start()
+        target[group] = source[group]
+
     def wait(sem, phase, target):
-        others = target.at[pl.ds(0, devices - 1)]
+        others = target.at[pl.ds(0, target.shape[0] - 1)]
         pltpu.make_async_copy(others, others, sem.at[phase]).wait()
 
     loads[0].wait()
@@ -162,14 +173,13 @@
     send(0, s_a, r_a)
     send(6, s_p, r_p, same=True)
 
-    row = lax.broadcasted_iota(jnp.int32, (8, plan.x), 0)
-    lane8 = lax.broadcasted_iota(jnp.int32, (8, plan.x), 1)
+    row = lax.broadcasted_iota(jnp.int32, (plan.res, plan.x), 0)
+    lane8 = lax.broadcasted_iota(jnp.int32, (plan.res, plan.x), 1)
     x = (lane8 >> 7) * plan.xl + (lane8 & 127)
-    r = me * plan.rl + lax.div(row & 3, plan.v2)
-    angle = (2.0 * math.pi / plan.width) * lax.rem(x * r, plan.width).astype(F32)
+    tw_c, tw_s = circle((x * (group * plan.res + row)) & (plan.width - 1), plan.width)
     scale = 1.0 / math.sqrt(plan.width)
-    tw_c = (jnp.cos(angle) * scale)[None]
-    tw_s = (jnp.sin(angle) * scale)[None]
+    tw_c = jnp.concatenate([tw_c * scale] * plan.cv, axis=0)
+    tw_s = jnp.concatenate([tw_s * scale] * plan.cv, axis=0)
 
     for load in loads[2:]:
         load.wait()
@@ -178,8 +188,8 @@
     data = r_a[...].astype(F32).reshape(half, 128).astype(BF16)
     total = jnp.dot(high[...], data, preferred_element_type=F32)
     total += jnp.dot(low[...], data, preferred_element_type=F32)
-    s_b[...] = total.reshape(devices, 8, 128)
-    send(1, s_b, r_b)
+    s_b[...] = total.reshape(plan.xg, plan.q, 128)
+    across(1, s_b, r_b)
 
     wait(recv_sem, 6, r_p)
     cell = (devices, 8, 128)
@@ -187,38 +197,38 @@
     in_tile = lax.broadcasted_iota(jnp.int32, cell, 2)
     for g in range(plan.xg):
         lanes = pl.ds(g * 128, 128)
-        tc, ts = circle((m * (in_tile + g * plan.xl)) & (SG - 1))
+        tc, ts = circle((m * (in_tile + g * plan.xl)) & (SG - 1), SG)
         tch[:, lanes], tcl[:, lanes] = split(tc.reshape(half, 128))
         tsh[:, lanes], tsl[:, lanes] = split(ts.reshape(half, 128))
 
     wait(recv_sem, 1, r_b)
 
-    got = r_b[...].reshape(plan.vg, plan.xg, 8, 128)
-    a = jnp.concatenate([got[:, g] for g in range(plan.xg)], axis=2)
+    a = jnp.concatenate([r_b[g] for g in range(plan.xg)], axis=1)
     a = a * tw_c + swapped(a) * tw_s
-    a_h, a_l = split(a.reshape(plan.q, plan.x))
-    w_h, w_l = split(swapped(a).reshape(plan.q, plan.x))
-    grid = nt(tch[...], jnp.concatenate([a_h, a_l], axis=0))
-    grid += nt(tsh[...], jnp.concatenate([w_h, w_l], axis=0))
-    grid = grid[:, : plan.q] + grid[:, plan.q :]
+    a_h, a_l = split(a)
+    w_h, w_l = split(swapped(a))
+    grid = nt(tch[...], a_h) + nt(tsh[...], w_h)
+    grid += nt(tch[...], a_l) + nt(tsh[...], w_l)
     grid += nt(tcl[...], a_h) + nt(tsl[...], w_h)
     s_c[...] = grid.reshape(devices, 8, plan.q).astype(BF16)
     send(2, s_c, r_c)
 
     cu = u_fine[...] // OVER
     shift = (KS - 1) / 2.0 + (u_fine[...] % OVER).astype(F32) / OVER
-    for i in range(plan.rl):
-        row = lax.broadcasted_iota(jnp.int32, (half, u_fine.shape[1]), 0)
-        cell = plan.nb * (row & 7) + (row >> 3) * plan.rl + i
-        offset = cell - cu
+    part = plan.xg * plan.res
+    for t in range(8):
+        row = lax.broadcasted_iota(jnp.int32, (part, u_fine.shape[1]), 0)
+        offset = row + plan.nb * t - cu
         distance = (offset.astype(F32) - shift) / 0.6
         weight = jnp.exp(-0.5 * distance * distance)
         weight = jnp.where((offset >= 0) & (offset < KS), weight, 0.0)
-        wu[pl.ds(i * half, half), :] = weight.astype(BF16)
-
-    shape = (plan.q, v_fine.shape[1])
+        wu[pl.ds(t * part, part), :] = weight.astype(BF16)
+
+    span = plan.vg * 8
+    shape = (plan.cv * span, v_fine.shape[1])
     row = lax.broadcasted_iota(jnp.int32, shape, 0)
-    offset = (row >> 3) * plan.v2 + lax.rem(row & 3, plan.v2) - v_fine[...] // OVER
+    v = lax.rem(lax.div(row, span), plan.v2) + lax.div(lax.rem(row, span), 8) * plan.v2
+    offset = v - v_fine[...] // OVER
     shift = (KS - 1) / 2.0 + (v_fine[...] % OVER).astype(F32) / OVER
     distance = (offset.astype(F32) - shift) / 0.6
     wv = jnp.exp(-0.5 * distance * distance)
@@ -226,41 +236,46 @@
 
     wait(recv_sem, 2, r_c)
 
-    cells = r_c[...].astype(F32).reshape(half, plan.q)
-    column = lax.broadcasted_iota(jnp.int32, (half, plan.q), 1)
-    residue = lax.div(column & 3, plan.v2)
-    parts = [jnp.where(residue == i, cells, 0.0) for i in range(plan.rl)]
-    cells = jnp.concatenate(parts, axis=0).astype(BF16)
-    along = tn(cells, wu[...]) * wv
-    along = jnp.sum(along.reshape(plan.vg, 8, -1), axis=0)
+    cells = r_c[...].astype(F32).reshape(plan.xg, span, plan.q)
+    cells = jnp.concatenate([cells[g] for g in range(plan.xg)], axis=1).T
+    cells = cells.reshape(plan.xg, plan.cv, plan.res, span)
+    cells = [cells[:, i].reshape(part, span) for i in range(plan.cv)]
+    cells = jnp.concatenate(cells, axis=1)
+    time = lax.broadcasted_iota(jnp.int32, cells.shape, 1) & 7
+    cells = jnp.concatenate([jnp.where(time == t, cells, 0.0) for t in range(8)], axis=0)
+    along = tn(cells.astype(BF16), wu[...]) * wv
+    middle = shape[0] // 2
     live = lax.broadcasted_iota(jnp.int32, (1, shape[1]), 1) < count[...]
-    real = jnp.where(live, observed[0] - jnp.sum(along[0:4], axis=0, keepdims=True), 0.0)
-    imag = jnp.where(live, observed[1] - jnp.sum(along[4:8], axis=0, keepdims=True), 0.0)
+    real = jnp.where(live, observed[0] - jnp.sum(along[:middle], axis=0, keepdims=True), 0.0)
+    imag = jnp.where(live, observed[1] - jnp.sum(along[middle:], axis=0, keepdims=True), 0.0)
     res[0] = real
     res[1] = imag
     kept = pltpu.make_async_copy(res, res_out, load_sem.at[0])
     kept.start()
     row = lax.broadcasted_iota(jnp.int32, shape, 0)
-    spread = (wv * jnp.where((row & 7) < 4, real, imag)).astype(BF16)
+    spread = (wv * jnp.where(row < middle, real, imag)).astype(BF16)
     both = nt(wu[...], spread)
-    regrid = both[0:half]
-    for i in range(1, plan.rl):
-        regrid = jnp.where(residue == i, both[i * half : (i + 1) * half], regrid)
+    regrid = both[:part]
+    for t in range(1, 8):
+        regrid = jnp.where(time == t, both[t * part : (t + 1) * part], regrid)
+    regrid = [regrid[:, i * span : (i + 1) * span] for i in range(plan.cv)]
+    regrid = [one.reshape(plan.xg, 1, plan.res, span) for one in regrid]
+    regrid = jnp.concatenate(regrid, axis=1).reshape(plan.xg * plan.q, span).T
+    regrid = [regrid[:, g * plan.q : (g + 1) * plan.q] for g in range(plan.xg)]
+    regrid = jnp.concatenate(regrid, axis=0)
     s_d[...] = regrid.reshape(devices, 8, plan.q).astype(BF16)
     send(3, s_d, r_d)
     wait(recv_sem, 3, r_d)
 
     cells = r_d[...].astype(F32).reshape(half, plan.q).astype(BF16)
-    first = tn(cells, tch[...]).reshape(plan.vg, 8, plan.x)
-    second = tn(cells, tsh[...]).reshape(plan.vg, 8, plan.x)
-    a = first - swapped(second)
+    a = tn(cells, tch[...]) - swapped(tn(cells, tsh[...]))
     a = a * tw_c - swapped(a) * tw_s
-    parts = [a[:, None, :, g * 128 : (g + 1) * 128] for g in range(plan.xg)]
-    s_e[...] = jnp.concatenate(parts, axis=1).reshape(devices, 8, 128).astype(BF16)
-    send(4, s_e, r_e)
+    for g in range(plan.xg):
+        s_e[g] = a[:, g * 128 : (g + 1) * 128].astype(BF16)
+    across(4, s_e, r_e)
     wait(recv_sem, 4, r_e)
 
-    data = r_e[...].astype(F32).reshape(half, 128).astype(BF16)
+    data = r_e[...].reshape(plan.xg * plan.q, 128)
     total = jnp.dot(back[...], data, preferred_element_type=F32)
     s_f[...] = total.reshape(devices, 8, 128).astype(BF16)
     send(5, s_f, r_f, local=True)
@@ -304,7 +319,8 @@
     high = table.astype(BF16)
     low = (table - high.astype(np.float32)).astype(BF16)
 
-    wide = pltpu.VMEM((devices, 8, 128), F32)
+    wide = pltpu.VMEM((plan.xg, plan.q, 128), F32)
+    narrow = pltpu.VMEM((plan.xg, plan.q, 128), BF16)
     tile = pltpu.VMEM((devices, 8, 128), BF16)
     cell = pltpu.VMEM((devices, 8, plan.q), BF16)
     turn = pltpu.VMEM((devices * 8, plan.x), BF16)
@@ -327,9 +343,9 @@
             tile, tile,
             pltpu.VMEM((1, 128), jnp.int32),
             pltpu.VMEM((devices, 1, 128), jnp.int32),
-            wide, wide, cell, cell, cell, cell, tile, tile, tile,
+            wide, wide, cell, cell, cell, cell, narrow, narrow, tile,
             pltpu.VMEM(vis_observed.shape, F32),
-            pltpu.VMEM((plan.rl * devices * 8, slots), BF16),
+            pltpu.VMEM((8 * plan.nb, slots), BF16),
             turn, turn, turn, turn,
             pltpu.SemaphoreType.DMA((7,)),
             pltpu.SemaphoreType.DMA((7,)),

time: 40.8 us -> 37.5 us (0.919)
  Pallas kernels: 38.7 us -> 35.4 us
    pallas_call x1, Pallas kernels: 37.1 us -> 33.8 us  [shards(): pl.pallas_call(functools.partial(kernel, plan), out_shape=(jax.ShapeDtype...]
where the time goes in v5:
time: 37.5 us; the launch traced here: 37.3 us
  Pallas kernels  35.4 us (94%)
  between operations  1.93 us (5%)
    pallas_call x1, Pallas kernels, shards(): pl.pallas_call(functools.partial(kernel, plan), out_shape=(jax.ShapeDtype...  33.8 us
    pallas_call x1, Pallas kernels, shards(): pl.pallas_call(functools.partial(finish, plan), out_shape=(jax.ShapeDtype...  1.55 us

profile of v5, /device:TPU:0, one launch (start us, length us, event | category | flops | bytes accessed | tf_op | source)
XLA Modules:
  0.0 37.3 jit_solution(14915080306340463639)
XLA Ops:
  1.9 33.8 %shard_map.104 = (f32[2,1,512]{2,1,0:T(1,128)}, bf16[32,8,128]{2,1,0:T(8,128)(2,1)}) custom-call(bf16[2,16,1024]{2,1,0:T(8,128)(2,1)} %refs_0_.1, s32[1,1]{1,0:T(1,128)} %bitcast.2.refs_1_, s32[1,512]{1,0:T(1,128)} %refs_2_.1, s32[1,512]{1,0:T(1,128)} %refs_3_.1, f32[2,1,512]{2,1,0:T(1,128)} %refs_4_.1, s32[1,1]{1,0:T(1,128)} %bitcast.3.refs_5_, ...), custom_call_target="tpu_custom_call" | custom-call | tf_op jit(solution)/shard_map/pallas_call | solution.py:332
  35.7 1.5 %shard_map.105 = (f32[2,1,512]{2,1,0:T(1,128)}, f32[2,16,1024]{2,1,0:T(8,128)}) custom-call(f32[2,1,512]{2,1,0:T(1,128)} %get-tuple-element.4.residual, bf16[32,8,128]{2,1,0:T(8,128)(2,1)} %get-tuple-element.5.got), custom_call_target="tpu_custom_call" | custom-call | tf_op jit(solution)/shard_map/pallas_call | solution.py:359

commit v6 on v5

--- a/solution.py
+++ b/solution.py
@@ -35,6 +35,8 @@
         self.cv = 2 * self.v2
         self.q = self.cv * self.res
         self.x = self.xg * 128
+        self.th = max(1, SG // self.nb // 4)
+        self.rows = self.th * devices * 4
         self.partners = sorted(range(1, devices), key=lambda i: -(i % nsub))
 
 
@@ -84,6 +86,25 @@
     return -cosine, -sine * h
 
 
+def to_rows(plan, a):
+    step = a.shape[0] // plan.th
+    return jnp.concatenate([a[h * step : (h + 1) * step] for h in range(plan.th)], axis=1)
+
+
+def to_slots(plan, a):
+    return to_rows(plan, a).reshape(plan.devices, 4, plan.th * plan.q)
+
+
+def from_slots(plan, a, groups):
+    a = a.astype(F32).reshape(plan.devices * 4, plan.th * plan.q)
+    step = a.shape[0] // groups
+    out = []
+    for g in range(groups):
+        for h in range(plan.th):
+            out.append(a[g * step : (g + 1) * step, h * plan.q : (h + 1) * plan.q])
+    return jnp.concatenate(out, axis=0)
+
+
 def rows(plan, c, k, v, g):
     return pl.ds(g * plan.vg * 8 + c * 4 + k * plan.v2 + v, plan.vg, stride=8)
 
@@ -192,14 +213,17 @@
     across(1, s_b, r_b)
 
     wait(recv_sem, 6, r_p)
-    cell = (devices, 8, 128)
-    m = r_p[...] + lax.broadcasted_iota(jnp.int32, cell, 1)
-    in_tile = lax.broadcasted_iota(jnp.int32, cell, 2)
-    for g in range(plan.xg):
-        lanes = pl.ds(g * 128, 128)
-        tc, ts = circle((m * (in_tile + g * plan.xl)) & (SG - 1), SG)
-        tch[:, lanes], tcl[:, lanes] = split(tc.reshape(half, 128))
-        tsh[:, lanes], tsl[:, lanes] = split(ts.reshape(half, 128))
+    base = jnp.broadcast_to(r_p[...], (devices, 4, 128)).reshape(devices * 4, 128)
+    base = base + (lax.broadcasted_iota(jnp.int32, base.shape, 0) & 3)
+    in_tile = lax.broadcasted_iota(jnp.int32, base.shape, 1)
+    for h in range(plan.th):
+        m = base + 4 * h
+        at = pl.ds(h * devices * 4, devices * 4)
+        for g in range(plan.xg):
+            lanes = pl.ds(g * 128, 128)
+            tc, ts = circle((m * (in_tile + g * plan.xl)) & (SG - 1), SG)
+            tch[at, lanes], tcl[at, lanes] = split(tc)
+            tsh[at, lanes], tsl[at, lanes] = split(ts)
 
     wait(recv_sem, 1, r_b)
 
@@ -210,13 +234,13 @@
     grid = nt(tch[...], a_h) + nt(tsh[...], w_h)
     grid += nt(tch[...], a_l) + nt(tsh[...], w_l)
     grid += nt(tcl[...], a_h) + nt(tsl[...], w_h)
-    s_c[...] = grid.reshape(devices, 8, plan.q).astype(BF16)
+    s_c[...] = to_slots(plan, grid).astype(BF16)
     send(2, s_c, r_c)
 
     cu = u_fine[...] // OVER
     shift = (KS - 1) / 2.0 + (u_fine[...] % OVER).astype(F32) / OVER
     part = plan.xg * plan.res
-    for t in range(8):
+    for t in range(4 * plan.th):
         row = lax.broadcasted_iota(jnp.int32, (part, u_fine.shape[1]), 0)
         offset = row + plan.nb * t - cu
         distance = (offset.astype(F32) - shift) / 0.6
@@ -224,10 +248,10 @@
         weight = jnp.where((offset >= 0) & (offset < KS), weight, 0.0)
         wu[pl.ds(t * part, part), :] = weight.astype(BF16)
 
-    span = plan.vg * 8
+    span = plan.th * plan.vg * 4
     shape = (plan.cv * span, v_fine.shape[1])
     row = lax.broadcasted_iota(jnp.int32, shape, 0)
-    v = lax.rem(lax.div(row, span), plan.v2) + lax.div(lax.rem(row, span), 8) * plan.v2
+    v = lax.rem(lax.div(row, span), plan.v2) + lax.rem(row >> 2, plan.vg) * plan.v2
     offset = v - v_fine[...] // OVER
     shift = (KS - 1) / 2.0 + (v_fine[...] % OVER).astype(F32) / OVER
     distance = (offset.astype(F32) - shift) / 0.6
@@ -236,13 +260,16 @@
 
     wait(recv_sem, 2, r_c)
 
-    cells = r_c[...].astype(F32).reshape(plan.xg, span, plan.q)
+    cells = from_slots(plan, r_c[...], plan.xg)
+    cells = cells.reshape(plan.xg, span, plan.q)
     cells = jnp.concatenate([cells[g] for g in range(plan.xg)], axis=1).T
     cells = cells.reshape(plan.xg, plan.cv, plan.res, span)
     cells = [cells[:, i].reshape(part, span) for i in range(plan.cv)]
     cells = jnp.concatenate(cells, axis=1)
-    time = lax.broadcasted_iota(jnp.int32, cells.shape, 1) & 7
-    cells = jnp.concatenate([jnp.where(time == t, cells, 0.0) for t in range(8)], axis=0)
+    place_in = lax.rem(lax.broadcasted_iota(jnp.int32, cells.shape, 1), span)
+    time = lax.div(place_in, plan.vg * 4) * 4 + (place_in & 3)
+    times = range(4 * plan.th)
+    cells = jnp.concatenate([jnp.where(time == t, cells, 0.0) for t in times], axis=0)
     along = tn(cells.astype(BF16), wu[...]) * wv
     middle = shape[0] // 2
     live = lax.broadcasted_iota(jnp.int32, (1, shape[1]), 1) < count[...]
@@ -256,18 +283,20 @@
     spread = (wv * jnp.where(row < middle, real, imag)).astype(BF16)
     both = nt(wu[...], spread)
     regrid = both[:part]
-    for t in range(1, 8):
+    for t in times[1:]:
         regrid = jnp.where(time == t, both[t * part : (t + 1) * part], regrid)
     regrid = [regrid[:, i * span : (i + 1) * span] for i in range(plan.cv)]
     regrid = [one.reshape(plan.xg, 1, plan.res, span) for one in regrid]
     regrid = jnp.concatenate(regrid, axis=1).reshape(plan.xg * plan.q, span).T
-    regrid = [regrid[:, g * plan.q : (g + 1) * plan.q] for g in range(plan.xg)]
+    regrid = [
+        to_rows(plan, regrid[:, g * plan.q : (g + 1) * plan.q]) for g in range(plan.xg)
+    ]
     regrid = jnp.concatenate(regrid, axis=0)
-    s_d[...] = regrid.reshape(devices, 8, plan.q).astype(BF16)
+    s_d[...] = regrid.reshape(devices, 4, plan.th * plan.q).astype(BF16)
     send(3, s_d, r_d)
     wait(recv_sem, 3, r_d)
 
-    cells = r_d[...].astype(F32).reshape(half, plan.q).astype(BF16)
+    cells = from_slots(plan, r_d[...], 1).astype(BF16)
     a = tn(cells, tch[...]) - swapped(tn(cells, tsh[...]))
     a = a * tw_c - swapped(a) * tw_s
     for g in range(plan.xg):
@@ -322,8 +351,8 @@
     wide = pltpu.VMEM((plan.xg, plan.q, 128), F32)
     narrow = pltpu.VMEM((plan.xg, plan.q, 128), BF16)
     tile = pltpu.VMEM((devices, 8, 128), BF16)
-    cell = pltpu.VMEM((devices, 8, plan.q), BF16)
-    turn = pltpu.VMEM((devices * 8, plan.x), BF16)
+    cell = pltpu.VMEM((devices, 4, plan.th * plan.q), BF16)
+    turn = pltpu.VMEM((plan.rows, plan.x), BF16)
     rows_v, columns = facet_data.shape[1:]
     operands = (
         facet_data, subgrid_pos.reshape(1, 1), vis_u_fine, vis_v_fine, vis_observed,
@@ -345,7 +374,7 @@
             pltpu.VMEM((devices, 1, 128), jnp.int32),
             wide, wide, cell, cell, cell, cell, narrow, narrow, tile,
             pltpu.VMEM(vis_observed.shape, F32),
-            pltpu.VMEM((8 * plan.nb, slots), BF16),
+            pltpu.VMEM((4 * plan.th * plan.nb, slots), BF16),
             turn, turn, turn, turn,
             pltpu.SemaphoreType.DMA((7,)),
             pltpu.SemaphoreType.DMA((7,)),

time: 37.5 us -> 37.6 us (level)
  no operation moved by 1% of the time
where the time goes in v6:
time: 37.6 us; the launch traced here: 37.4 us
  Pallas kernels  35.5 us (94%)
  between operations  1.93 us (5%)
    pallas_call x1, Pallas kernels, shards(): pl.pallas_call(functools.partial(kernel, plan), out_shape=(jax.ShapeDtype...  33.9 us
    pallas_call x1, Pallas kernels, shards(): pl.pallas_call(functools.partial(finish, plan), out_shape=(jax.ShapeDtype...  1.55 us

profile of v6, /device:TPU:0, one launch (start us, length us, event | category | flops | bytes accessed | tf_op | source)
XLA Modules:
  0.0 37.4 jit_solution(16837622773274466390)
XLA Ops:
  1.9 33.9 %shard_map.104 = (f32[2,1,512]{2,1,0:T(1,128)}, bf16[32,8,128]{2,1,0:T(8,128)(2,1)}) custom-call(bf16[2,16,1024]{2,1,0:T(8,128)(2,1)} %refs_0_.1, s32[1,1]{1,0:T(1,128)} %bitcast.2.refs_1_, s32[1,512]{1,0:T(1,128)} %refs_2_.1, s32[1,512]{1,0:T(1,128)} %refs_3_.1, f32[2,1,512]{2,1,0:T(1,128)} %refs_4_.1, s32[1,1]{1,0:T(1,128)} %bitcast.3.refs_5_, ...), custom_call_target="tpu_custom_call" | custom-call | tf_op jit(solution)/shard_map/pallas_call | solution.py:361
  35.8 1.5 %shard_map.105 = (f32[2,1,512]{2,1,0:T(1,128)}, f32[2,16,1024]{2,1,0:T(8,128)}) custom-call(f32[2,1,512]{2,1,0:T(1,128)} %get-tuple-element.4.residual, bf16[32,8,128]{2,1,0:T(8,128)(2,1)} %get-tuple-element.5.got), custom_call_target="tpu_custom_call" | custom-call | tf_op jit(solution)/shard_map/pallas_call | solution.py:388

commit v7 on v6

--- a/solution.py
+++ b/solution.py
@@ -112,10 +112,10 @@
 def kernel(plan, *refs):
     operands, (res_out, r_f) = refs[:9], refs[9:11]
     (
-        image, slots, s_a, r_a, s_p, r_p, s_b, r_b, s_c, r_c, s_d, r_d, s_e, r_e, s_f,
+        image, slots, s_a, r_a, s_p, g_p, r_p, s_b, r_b, s_c, r_c, s_d, r_d, s_e, r_e, s_f,
         res, wu, tch, tcl, tsh, tsl, send_sem, recv_sem, load_sem,
-    ) = refs[11:35]
-    held = refs[35:]
+    ) = refs[11:36]
+    held = refs[36:]
     facet, position, u_fine, v_fine, observed, count, high, low, back = held
     devices, nsub = plan.devices, plan.nsub
     group, column = lax.axis_index("facet"), lax.axis_index("sub")
@@ -137,11 +137,11 @@
     for i in plan.partners:
         pl.semaphore_signal(barrier, inc=1, device_id=place(i)[1], device_id_type=MESH)
 
-    def send(phase, source, target, same=False, local=False):
+    def send(phase, source, target, local=False):
         for i in plan.partners:
             to, device = place(i)
             pltpu.make_async_remote_copy(
-                src_ref=source if same else source.at[to],
+                src_ref=source.at[to],
                 dst_ref=target.at[me],
                 send_sem=send_sem.at[phase],
                 recv_sem=recv_sem.at[phase],
@@ -149,7 +149,19 @@
                 device_id_type=MESH,
             ).start()
         if not local:
-            target[me] = source[...] if same else source[me]
+            target[me] = source[me]
+
+    def share(phase, source, target, own, partners):
+        for device in partners:
+            pltpu.make_async_remote_copy(
+                src_ref=source,
+                dst_ref=target.at[own],
+                send_sem=send_sem.at[phase],
+                recv_sem=recv_sem.at[phase],
+                device_id=device,
+                device_id_type=MESH,
+            ).start()
+        target[own] = source[...]
 
     def across(phase, source, target):
         for i in range(1, plan.xg):
@@ -191,8 +203,10 @@
     s_p[...] = jnp.broadcast_to(position[...] // plan.nb, s_p.shape)
 
     pl.semaphore_wait(barrier, devices - 1)
+    share(6, s_p, g_p, group, [(group ^ i, column) for i in range(1, plan.xg)])
     send(0, s_a, r_a)
-    send(6, s_p, r_p, same=True)
+    wait(recv_sem, 6, g_p)
+    share(7, g_p, r_p, column, [(group, column ^ i) for i in range(1, nsub)])
 
     row = lax.broadcasted_iota(jnp.int32, (plan.res, plan.x), 0)
     lane8 = lax.broadcasted_iota(jnp.int32, (plan.res, plan.x), 1)
@@ -212,8 +226,9 @@
     s_b[...] = total.reshape(plan.xg, plan.q, 128)
     across(1, s_b, r_b)
 
-    wait(recv_sem, 6, r_p)
-    base = jnp.broadcast_to(r_p[...], (devices, 4, 128)).reshape(devices * 4, 128)
+    wait(recv_sem, 7, r_p)
+    base = jnp.concatenate([r_p[:, g] for g in range(plan.xg)], axis=0)
+    base = jnp.broadcast_to(base, (devices, 4, 128)).reshape(devices * 4, 128)
     base = base + (lax.broadcasted_iota(jnp.int32, base.shape, 0) & 3)
     in_tile = lax.broadcasted_iota(jnp.int32, base.shape, 1)
     for h in range(plan.th):
@@ -314,7 +329,7 @@
     own.wait()
     kept.wait()
 
-    for phase, sent in enumerate((r_a, r_b, r_c, r_d, r_e, r_f, r_p)):
+    for phase, sent in enumerate((r_a, r_b, r_c, r_d, r_e, r_f, g_p, r_p)):
         wait(send_sem, phase, sent)
 
 
@@ -371,13 +386,14 @@
             pltpu.VMEM((devices * 8, 128), F32),
             tile, tile,
             pltpu.VMEM((1, 128), jnp.int32),
-            pltpu.VMEM((devices, 1, 128), jnp.int32),
+            pltpu.VMEM((plan.xg, 1, 128), jnp.int32),
+            pltpu.VMEM((nsub, plan.xg, 1, 128), jnp.int32),
             wide, wide, cell, cell, cell, cell, narrow, narrow, tile,
             pltpu.VMEM(vis_observed.shape, F32),
             pltpu.VMEM((4 * plan.th * plan.nb, slots), BF16),
             turn, turn, turn, turn,
-            pltpu.SemaphoreType.DMA((7,)),
-            pltpu.SemaphoreType.DMA((7,)),
+            pltpu.SemaphoreType.DMA((8,)),
+            pltpu.SemaphoreType.DMA((8,)),
             pltpu.SemaphoreType.DMA((9,)),
         ]
         + [pltpu.VMEM(one.shape, one.dtype) for one in operands],

time: 37.6 us -> 37.7 us (level)
  no operation moved by 1% of the time
where the time goes in v7:
time: 37.7 us; the launch traced here: 37.6 us
  Pallas kernels  35.6 us (94%)
  between operations  1.93 us (5%)
    pallas_call x1, Pallas kernels, shards(): pl.pallas_call(functools.partial(kernel, plan), out_shape=(jax.ShapeDtype...  34.1 us
    pallas_call x1, Pallas kernels, shards(): pl.pallas_call(functools.partial(finish, plan), out_shape=(jax.ShapeDtype...  1.55 us

profile of v7, /device:TPU:0, one launch (start us, length us, event | category | flops | bytes accessed | tf_op | source)
XLA Modules:
  0.0 37.6 jit_solution(3780325562119239291)
XLA Ops:
  1.9 34.1 %shard_map.104 = (f32[2,1,512]{2,1,0:T(1,128)}, bf16[32,8,128]{2,1,0:T(8,128)(2,1)}) custom-call(bf16[2,16,1024]{2,1,0:T(8,128)(2,1)} %refs_0_.1, s32[1,1]{1,0:T(1,128)} %bitcast.2.refs_1_, s32[1,512]{1,0:T(1,128)} %refs_2_.1, s32[1,512]{1,0:T(1,128)} %refs_3_.1, f32[2,1,512]{2,1,0:T(1,128)} %refs_4_.1, s32[1,1]{1,0:T(1,128)} %bitcast.3.refs_5_, ...), custom_call_target="tpu_custom_call" | custom-call | tf_op jit(solution)/shard_map/pallas_call | solution.py:376
  36.0 1.5 %shard_map.105 = (f32[2,1,512]{2,1,0:T(1,128)}, f32[2,16,1024]{2,1,0:T(8,128)}) custom-call(f32[2,1,512]{2,1,0:T(1,128)} %get-tuple-element.4.residual, bf16[32,8,128]{2,1,0:T(8,128)(2,1)} %get-tuple-element.5.got), custom_call_target="tpu_custom_call" | custom-call | tf_op jit(solution)/shard_map/pallas_call | solution.py:404

commit v8 on v6

--- a/solution.py
+++ b/solution.py
@@ -231,8 +231,9 @@
     a = a * tw_c + swapped(a) * tw_s
     a_h, a_l = split(a)
     w_h, w_l = split(swapped(a))
-    grid = nt(tch[...], a_h) + nt(tsh[...], w_h)
-    grid += nt(tch[...], a_l) + nt(tsh[...], w_l)
+    grid = nt(tch[...], jnp.concatenate([a_h, a_l], axis=0))
+    grid += nt(tsh[...], jnp.concatenate([w_h, w_l], axis=0))
+    grid = grid[:, : plan.q] + grid[:, plan.q :]
     grid += nt(tcl[...], a_h) + nt(tsl[...], w_h)
     s_c[...] = to_slots(plan, grid).astype(BF16)
     send(2, s_c, r_c)

time: 37.6 us -> 37 us (0.984)
  Pallas kernels: 35.5 us -> 34.9 us
    pallas_call x1, Pallas kernels: 33.9 us -> 33.3 us  [shards(): pl.pallas_call(functools.partial(kernel, plan), out_shape=(jax.ShapeDtype...]
where the time goes in v8:
time: 37 us; the launch traced here: 36.8 us
  Pallas kernels  34.9 us (94%)
  between operations  1.93 us (5%)
    pallas_call x1, Pallas kernels, shards(): pl.pallas_call(functools.partial(kernel, plan), out_shape=(jax.ShapeDtype...  33.3 us
    pallas_call x1, Pallas kernels, shards(): pl.pallas_call(functools.partial(finish, plan), out_shape=(jax.ShapeDtype...  1.55 us

profile of v8, /device:TPU:0, one launch (start us, length us, event | category | flops | bytes accessed | tf_op | source)
XLA Modules:
  0.0 36.8 jit_solution(7587159536597084147)
XLA Ops:
  1.9 33.3 %shard_map.104 = (f32[2,1,512]{2,1,0:T(1,128)}, bf16[32,8,128]{2,1,0:T(8,128)(2,1)}) custom-call(bf16[2,16,1024]{2,1,0:T(8,128)(2,1)} %refs_0_.1, s32[1,1]{1,0:T(1,128)} %bitcast.2.refs_1_, s32[1,512]{1,0:T(1,128)} %refs_2_.1, s32[1,512]{1,0:T(1,128)} %refs_3_.1, f32[2,1,512]{2,1,0:T(1,128)} %refs_4_.1, s32[1,1]{1,0:T(1,128)} %bitcast.3.refs_5_, ...), custom_call_target="tpu_custom_call" | custom-call | tf_op jit(solution)/shard_map/pallas_call | solution.py:362
  35.3 1.5 %shard_map.105 = (f32[2,1,512]{2,1,0:T(1,128)}, f32[2,16,1024]{2,1,0:T(8,128)}) custom-call(f32[2,1,512]{2,1,0:T(1,128)} %get-tuple-element.4.residual, bf16[32,8,128]{2,1,0:T(8,128)(2,1)} %get-tuple-element.5.got), custom_call_target="tpu_custom_call" | custom-call | tf_op jit(solution)/shard_map/pallas_call | solution.py:389
